TPU v7x, 32 devices: a whole 2x2x4 slice. The times are simulated.
32 devices in a mesh: parts: 2 (over y), xy: 4 (over z), gz: 4 (over x, core).
Axes of the slice: x: 2, y: 2, z: 4, core: 2. Of those that a mesh axis runs over, the one named last changes fastest.
Arguments:
- features: bfloat16 [96, 65536], P(None, ('parts', 'xy', 'gz')), parts along dimension 1, may hold values from -6 to 6
- weight: bfloat16 [27, 96, 96], replicated, may hold values from -0.15625 to 0.15625
- z_send: int32 [8, 4, 512], P(('parts', 'xy'), 'gz'), parts along dimension 0, may hold values from -1 to 2047, as said below
- xy_send: int32 [8, 4, 1024], P(('parts', 'xy'), 'gz'), parts along dimension 0, may hold values from -1 to 2559, as said below
- kernel_map: int32 [27, 65536], P(None, ('parts', 'xy', 'gz')), parts along dimension 1, may hold values from -1 to 3583, as said below
- cotangent: bfloat16 [96, 65536], P(None, ('parts', 'xy', 'gz')), parts along dimension 1, may hold values from -6 to 6
Outputs:
- out_features: bfloat16 [96, 65536], P(None, ('parts', 'xy', 'gz')), parts along dimension 1
- grad_features: float32 [96, 65536], P(None, ('parts', 'xy', 'gz')), parts along dimension 1
- grad_weight: float32 [192, 2592], P(('parts', 'xy')), parts along dimension 0
There are 2 independent parts, one for each index of `parts`. A program takes and returns all parts, laid end to end along the dimension named above; an argument that names none is the same for every part. Nothing has to cross between parts.
Inputs may be any that keep to these rules, and one draw needn't show every extreme that they name: `z_send`: slots of the device's own active voxels; the first 256 entries go to the layer below, the last 256 to the layer above; -1 marks an unused entry. `xy_send`: columns of the device's extended matrix; entries p * 256 to (p + 1) * 256 - 1 go to xy peer p; -1 marks an unused entry. `kernel_map`: column of the owning device's table; -1 where the offset has no active voxel or the slot is inactive; offset 27 // 2 of an active slot names that slot itself.
All inputs are finite; a program needn't handle non-finite values.
Results may differ from a plain program's by a relative error of at most 0.002.
Values may be sent and summed in bfloat16 or wider, within the bound.
A program may use at most 64 MiB of HBM per device.

v0:
```python
import math

import jax
import jax.numpy as jnp
from jax import lax
from jax.sharding import PartitionSpec as P


def padded_2(block, sides, width):
    for axis, dim in sides:
        count = lax.axis_size(axis)
        forward = [(i, i + 1) for i in range(count - 1)]
        backward = [(target, source) for source, target in forward]
        low = lax.ppermute(
            lax.slice_in_dim(block, block.shape[dim] - width, None, axis=dim), axis, forward
        )
        high = lax.ppermute(lax.slice_in_dim(block, 0, width, axis=dim), axis, backward)
        block = jnp.concatenate([low, block, high], axis=dim)
    return block


def pick_rows(row_table, row_index):
    table_rows = row_table.shape[0]
    padded = jnp.concatenate(
        [row_table, jnp.zeros((1, row_table.shape[1]), row_table.dtype)], axis=0
    )
    safe_index = jnp.where(row_index < 0, table_rows, row_index)
    return jnp.take(padded, safe_index, axis=0)


def add_rows(base_grad, row_index, values):
    table_rows = base_grad.shape[0]
    padded = jnp.concatenate(
        [base_grad, jnp.zeros((1, base_grad.shape[1]), base_grad.dtype)], axis=0
    )
    safe_index = jnp.where(row_index < 0, table_rows, row_index)
    return padded.at[safe_index].add(values)[:table_rows]


def on_device(features, weight, z_send, xy_send, kernel_map, cotangent):
    channels, slots = features.shape
    offsets = weight.shape[0]
    peer_count = lax.axis_size("xy")
    z_list = z_send.reshape(-1)
    xy_list = xy_send.reshape(-1)
    rim_width = z_list.shape[0] // 2
    per_peer = xy_list.shape[0] // peer_count
    feature_rows = features.T
    upstream_rows = cotangent.T
    outgoing = pick_rows(feature_rows, z_list)
    widened = padded_2(outgoing, (("gz", 0),), rim_width)
    from_below = widened[:rim_width]
    from_above = widened[widened.shape[0] - rim_width :]
    extended = jnp.concatenate([feature_rows, from_below, from_above], axis=0)
    send_blocks = pick_rows(extended, xy_list).reshape(peer_count, per_peer, channels)
    received = lax.all_to_all(send_blocks, "xy", split_axis=0, concat_axis=0, tiled=True)
    voxel_table = jnp.concatenate(
        [extended, received.reshape(peer_count * per_peer, channels)], axis=0
    )
    table_rows = voxel_table.shape[0]
    padded_table = jnp.concatenate(
        [voxel_table, jnp.zeros((1, channels), voxel_table.dtype)], axis=0
    )
    zero_index = jnp.zeros((), jnp.int32)

    def offset_step(offset, loop_state):
        out_rows, grad_padded, w_grad = loop_state
        row_index = lax.dynamic_index_in_dim(kernel_map, offset, 0, keepdims=False)
        w_offset = lax.dynamic_index_in_dim(weight, offset, 0, keepdims=False)
        safe_index = jnp.where(row_index < 0, table_rows, row_index)
        gathered = jnp.take(padded_table, safe_index, axis=0)
        out_rows = out_rows + jnp.dot(gathered, w_offset, preferred_element_type=jnp.float32)
        back_grad = lax.dot_general(
            upstream_rows, w_offset, (((1,), (1,)), ((), ())), preferred_element_type=jnp.float32
        )
        grad_padded = grad_padded.at[safe_index].add(back_grad)
        w_piece = jnp.dot(cotangent, gathered, preferred_element_type=jnp.float32)
        w_grad = lax.dynamic_update_slice(
            w_grad, w_piece[:, None, :], (zero_index, offset, zero_index)
        )
        return (out_rows, grad_padded, w_grad)

    start_state = (
        jnp.zeros((slots, channels), jnp.float32),
        jnp.zeros((table_rows + 1, channels), jnp.float32),
        jnp.zeros((channels, offsets, channels), jnp.float32),
    )
    out_rows, grad_padded, w_grad = lax.fori_loop(0, offsets, offset_step, start_state)
    out_features = out_rows.T.astype(jnp.bfloat16)
    w_scale = 1.0 / math.sqrt(slots * peer_count * lax.axis_size("gz"))
    w_term = w_grad.reshape(channels, offsets * channels)
    row_count = channels // peer_count
    w_total = lax.psum(w_term, ("xy", "gz"))
    w_mine = lax.dynamic_slice_in_dim(w_total, lax.axis_index("xy") * row_count, row_count, 0)
    grad_weight = w_mine * w_scale
    ext_width = slots + 2 * rim_width
    grad_recv = grad_padded[ext_width:table_rows].reshape(peer_count, per_peer, channels)
    returned = lax.all_to_all(
        grad_recv.astype(jnp.bfloat16), "xy", split_axis=0, concat_axis=0, tiled=True
    ).astype(grad_recv.dtype)
    grad_ext = add_rows(
        grad_padded[:ext_width], xy_list, returned.reshape(peer_count * per_peer, channels)
    )
    z_grads = grad_ext[slots:]
    wide_grads = padded_2(z_grads.astype(jnp.bfloat16), (("gz", 0),), rim_width).astype(
        z_grads.dtype
    )
    grad_outgoing = jnp.concatenate(
        [wide_grads[:rim_width], wide_grads[wide_grads.shape[0] - rim_width :]], axis=0
    )
    grad_rows = add_rows(grad_ext[:slots], z_list, grad_outgoing)
    grad_features = grad_rows.T
    return (out_features, grad_features, grad_weight)


def solution(mesh):
    in_specs = (
        P(None, ("parts", "xy", "gz")),
        P(),
        P(("parts", "xy"), "gz", None),
        P(("parts", "xy"), "gz", None),
        P(None, ("parts", "xy", "gz")),
        P(None, ("parts", "xy", "gz")),
    )
    out_specs = (
        P(None, ("parts", "xy", "gz")),
        P(None, ("parts", "xy", "gz")),
        P(("parts", "xy"), None),
    )
    return jax.shard_map(
        on_device, mesh=mesh, in_specs=in_specs, out_specs=out_specs, check_vma=False
    )
```

profile of v0, /device:TPU:17, one launch (start us, length us, event | category | flops | bytes accessed | tf_op | source)
XLA Modules:
  0.0 883.5 jit_solution(4783279957809001341)
XLA Ops:
  11.5 3.7 collective-permute-start
  20.9 3.2 gather_fusion.2
  25.0 4.6 all-to-all-start
  33.4 701.6 %while.18 = (s32[]{:T(128)}, f32[2048,96]{0,1:T(8,128)}, f32[3585,96]{1,0:T(8,128)S(1)}, f32[96,27,96]{0,2,1:T(8,128)}, s32[27,2048]{1,0:T(8,128)}, /*index=5*/b...) while((s32[]{:T(128)}, f32[2048,96]{0,1:T(8,128)}, ...), condition=%wide.region_2.3_spmd.clone, body=%wide.region_0.2_spmd.clone.sunk | while | flops 114257920 | bytes 11968179 | solution.py:88
  34.3 6.2 gather_fusion
  46.4 12.6 %scatter_fusion = f32[3585,96]{1,0:T(8,128)S(1)} fusion(f32[3585,96]{1,0:T(8,128)S(1)} %get-tuple-element.299, s32[2048]{0:T(1024)S(1)} %bitcast.61, f32[2048,96]{1,0:T(8,128)} %copy.43), kind=kCustom, calls=%fused_computation.3.clone.clone.1 | custom fusion | flops 196608 | bytes 2367488 | tf_op jit(solution)/shard_map/while/body/eval_jaxpr/scatter-add | solution.py:76
  59.9 6.2 gather_fusion
  72.4 12.6 %scatter_fusion = f32[3585,96]{1,0:T(8,128)S(1)} fusion(f32[3585,96]{1,0:T(8,128)S(1)} %get-tuple-element.299, s32[2048]{0:T(1024)S(1)} %bitcast.61, f32[2048,96]{1,0:T(8,128)} %copy.43), kind=kCustom, calls=%fused_computation.3.clone.clone.1 | custom fusion | flops 196608 | bytes 2367488 | tf_op jit(solution)/shard_map/while/body/eval_jaxpr/scatter-add | solution.py:76
  85.9 6.2 gather_fusion
  98.4 12.6 %scatter_fusion = f32[3585,96]{1,0:T(8,128)S(1)} fusion(f32[3585,96]{1,0:T(8,128)S(1)} %get-tuple-element.299, s32[2048]{0:T(1024)S(1)} %bitcast.61, f32[2048,96]{1,0:T(8,128)} %copy.43), kind=kCustom, calls=%fused_computation.3.clone.clone.1 | custom fusion | flops 196608 | bytes 2367488 | tf_op jit(solution)/shard_map/while/body/eval_jaxpr/scatter-add | solution.py:76
  111.9 6.2 gather_fusion
  124.4 12.6 %scatter_fusion = f32[3585,96]{1,0:T(8,128)S(1)} fusion(f32[3585,96]{1,0:T(8,128)S(1)} %get-tuple-element.299, s32[2048]{0:T(1024)S(1)} %bitcast.61, f32[2048,96]{1,0:T(8,128)} %copy.43), kind=kCustom, calls=%fused_computation.3.clone.clone.1 | custom fusion | flops 196608 | bytes 2367488 | tf_op jit(solution)/shard_map/while/body/eval_jaxpr/scatter-add | solution.py:76
  137.9 6.2 gather_fusion
  150.4 12.6 %scatter_fusion = f32[3585,96]{1,0:T(8,128)S(1)} fusion(f32[3585,96]{1,0:T(8,128)S(1)} %get-tuple-element.299, s32[2048]{0:T(1024)S(1)} %bitcast.61, f32[2048,96]{1,0:T(8,128)} %copy.43), kind=kCustom, calls=%fused_computation.3.clone.clone.1 | custom fusion | flops 196608 | bytes 2367488 | tf_op jit(solution)/shard_map/while/body/eval_jaxpr/scatter-add | solution.py:76
  163.9 6.2 gather_fusion
  176.4 12.6 %scatter_fusion = f32[3585,96]{1,0:T(8,128)S(1)} fusion(f32[3585,96]{1,0:T(8,128)S(1)} %get-tuple-element.299, s32[2048]{0:T(1024)S(1)} %bitcast.61, f32[2048,96]{1,0:T(8,128)} %copy.43), kind=kCustom, calls=%fused_computation.3.clone.clone.1 | custom fusion | flops 196608 | bytes 2367488 | tf_op jit(solution)/shard_map/while/body/eval_jaxpr/scatter-add | solution.py:76
  189.9 6.2 gather_fusion
  202.4 12.6 %scatter_fusion = f32[3585,96]{1,0:T(8,128)S(1)} fusion(f32[3585,96]{1,0:T(8,128)S(1)} %get-tuple-element.299, s32[2048]{0:T(1024)S(1)} %bitcast.61, f32[2048,96]{1,0:T(8,128)} %copy.43), kind=kCustom, calls=%fused_computation.3.clone.clone.1 | custom fusion | flops 196608 | bytes 2367488 | tf_op jit(solution)/shard_map/while/body/eval_jaxpr/scatter-add | solution.py:76
  215.9 6.2 gather_fusion
  228.4 12.6 %scatter_fusion = f32[3585,96]{1,0:T(8,128)S(1)} fusion(f32[3585,96]{1,0:T(8,128)S(1)} %get-tuple-element.299, s32[2048]{0:T(1024)S(1)} %bitcast.61, f32[2048,96]{1,0:T(8,128)} %copy.43), kind=kCustom, calls=%fused_computation.3.clone.clone.1 | custom fusion | flops 196608 | bytes 2367488 | tf_op jit(solution)/shard_map/while/body/eval_jaxpr/scatter-add | solution.py:76
  241.9 6.2 gather_fusion
  254.4 12.6 %scatter_fusion = f32[3585,96]{1,0:T(8,128)S(1)} fusion(f32[3585,96]{1,0:T(8,128)S(1)} %get-tuple-element.299, s32[2048]{0:T(1024)S(1)} %bitcast.61, f32[2048,96]{1,0:T(8,128)} %copy.43), kind=kCustom, calls=%fused_computation.3.clone.clone.1 | custom fusion | flops 196608 | bytes 2367488 | tf_op jit(solution)/shard_map/while/body/eval_jaxpr/scatter-add | solution.py:76
  267.9 6.2 gather_fusion
  280.4 12.6 %scatter_fusion = f32[3585,96]{1,0:T(8,128)S(1)} fusion(f32[3585,96]{1,0:T(8,128)S(1)} %get-tuple-element.299, s32[2048]{0:T(1024)S(1)} %bitcast.61, f32[2048,96]{1,0:T(8,128)} %copy.43), kind=kCustom, calls=%fused_computation.3.clone.clone.1 | custom fusion | flops 196608 | bytes 2367488 | tf_op jit(solution)/shard_map/while/body/eval_jaxpr/scatter-add | solution.py:76
  293.9 6.2 gather_fusion
  306.4 12.6 %scatter_fusion = f32[3585,96]{1,0:T(8,128)S(1)} fusion(f32[3585,96]{1,0:T(8,128)S(1)} %get-tuple-element.299, s32[2048]{0:T(1024)S(1)} %bitcast.61, f32[2048,96]{1,0:T(8,128)} %copy.43), kind=kCustom, calls=%fused_computation.3.clone.clone.1 | custom fusion | flops 196608 | bytes 2367488 | tf_op jit(solution)/shard_map/while/body/eval_jaxpr/scatter-add | solution.py:76
  319.9 6.2 gather_fusion
  332.4 12.6 %scatter_fusion = f32[3585,96]{1,0:T(8,128)S(1)} fusion(f32[3585,96]{1,0:T(8,128)S(1)} %get-tuple-element.299, s32[2048]{0:T(1024)S(1)} %bitcast.61, f32[2048,96]{1,0:T(8,128)} %copy.43), kind=kCustom, calls=%fused_computation.3.clone.clone.1 | custom fusion | flops 196608 | bytes 2367488 | tf_op jit(solution)/shard_map/while/body/eval_jaxpr/scatter-add | solution.py:76
  345.9 6.2 gather_fusion
  358.4 12.6 %scatter_fusion = f32[3585,96]{1,0:T(8,128)S(1)} fusion(f32[3585,96]{1,0:T(8,128)S(1)} %get-tuple-element.299, s32[2048]{0:T(1024)S(1)} %bitcast.61, f32[2048,96]{1,0:T(8,128)} %copy.43), kind=kCustom, calls=%fused_computation.3.clone.clone.1 | custom fusion | flops 196608 | bytes 2367488 | tf_op jit(solution)/shard_map/while/body/eval_jaxpr/scatter-add | solution.py:76
  371.9 6.2 gather_fusion
  384.4 12.6 %scatter_fusion = f32[3585,96]{1,0:T(8,128)S(1)} fusion(f32[3585,96]{1,0:T(8,128)S(1)} %get-tuple-element.299, s32[2048]{0:T(1024)S(1)} %bitcast.61, f32[2048,96]{1,0:T(8,128)} %copy.43), kind=kCustom, calls=%fused_computation.3.clone.clone.1 | custom fusion | flops 196608 | bytes 2367488 | tf_op jit(solution)/shard_map/while/body/eval_jaxpr/scatter-add | solution.py:76
  397.9 6.2 gather_fusion
  410.4 12.6 %scatter_fusion = f32[3585,96]{1,0:T(8,128)S(1)} fusion(f32[3585,96]{1,0:T(8,128)S(1)} %get-tuple-element.299, s32[2048]{0:T(1024)S(1)} %bitcast.61, f32[2048,96]{1,0:T(8,128)} %copy.43), kind=kCustom, calls=%fused_computation.3.clone.clone.1 | custom fusion | flops 196608 | bytes 2367488 | tf_op jit(solution)/shard_map/while/body/eval_jaxpr/scatter-add | solution.py:76
  423.9 6.2 gather_fusion
  436.4 12.6 %scatter_fusion = f32[3585,96]{1,0:T(8,128)S(1)} fusion(f32[3585,96]{1,0:T(8,128)S(1)} %get-tuple-element.299, s32[2048]{0:T(1024)S(1)} %bitcast.61, f32[2048,96]{1,0:T(8,128)} %copy.43), kind=kCustom, calls=%fused_computation.3.clone.clone.1 | custom fusion | flops 196608 | bytes 2367488 | tf_op jit(solution)/shard_map/while/body/eval_jaxpr/scatter-add | solution.py:76
  449.9 6.2 gather_fusion
  462.4 12.6 %scatter_fusion = f32[3585,96]{1,0:T(8,128)S(1)} fusion(f32[3585,96]{1,0:T(8,128)S(1)} %get-tuple-element.299, s32[2048]{0:T(1024)S(1)} %bitcast.61, f32[2048,96]{1,0:T(8,128)} %copy.43), kind=kCustom, calls=%fused_computation.3.clone.clone.1 | custom fusion | flops 196608 | bytes 2367488 | tf_op jit(solution)/shard_map/while/body/eval_jaxpr/scatter-add | solution.py:76
  475.9 6.2 gather_fusion
  488.4 12.6 %scatter_fusion = f32[3585,96]{1,0:T(8,128)S(1)} fusion(f32[3585,96]{1,0:T(8,128)S(1)} %get-tuple-element.299, s32[2048]{0:T(1024)S(1)} %bitcast.61, f32[2048,96]{1,0:T(8,128)} %copy.43), kind=kCustom, calls=%fused_computation.3.clone.clone.1 | custom fusion | flops 196608 | bytes 2367488 | tf_op jit(solution)/shard_map/while/body/eval_jaxpr/scatter-add | solution.py:76
  501.9 6.2 gather_fusion
  514.4 12.6 %scatter_fusion = f32[3585,96]{1,0:T(8,128)S(1)} fusion(f32[3585,96]{1,0:T(8,128)S(1)} %get-tuple-element.299, s32[2048]{0:T(1024)S(1)} %bitcast.61, f32[2048,96]{1,0:T(8,128)} %copy.43), kind=kCustom, calls=%fused_computation.3.clone.clone.1 | custom fusion | flops 196608 | bytes 2367488 | tf_op jit(solution)/shard_map/while/body/eval_jaxpr/scatter-add | solution.py:76
  527.9 6.2 gather_fusion
  540.4 12.6 %scatter_fusion = f32[3585,96]{1,0:T(8,128)S(1)} fusion(f32[3585,96]{1,0:T(8,128)S(1)} %get-tuple-element.299, s32[2048]{0:T(1024)S(1)} %bitcast.61, f32[2048,96]{1,0:T(8,128)} %copy.43), kind=kCustom, calls=%fused_computation.3.clone.clone.1 | custom fusion | flops 196608 | bytes 2367488 | tf_op jit(solution)/shard_map/while/body/eval_jaxpr/scatter-add | solution.py:76
  553.9 6.2 gather_fusion
  566.4 12.6 %scatter_fusion = f32[3585,96]{1,0:T(8,128)S(1)} fusion(f32[3585,96]{1,0:T(8,128)S(1)} %get-tuple-element.299, s32[2048]{0:T(1024)S(1)} %bitcast.61, f32[2048,96]{1,0:T(8,128)} %copy.43), kind=kCustom, calls=%fused_computation.3.clone.clone.1 | custom fusion | flops 196608 | bytes 2367488 | tf_op jit(solution)/shard_map/while/body/eval_jaxpr/scatter-add | solution.py:76
  579.9 6.2 gather_fusion
  592.4 12.6 %scatter_fusion = f32[3585,96]{1,0:T(8,128)S(1)} fusion(f32[3585,96]{1,0:T(8,128)S(1)} %get-tuple-element.299, s32[2048]{0:T(1024)S(1)} %bitcast.61, f32[2048,96]{1,0:T(8,128)} %copy.43), kind=kCustom, calls=%fused_computation.3.clone.clone.1 | custom fusion | flops 196608 | bytes 2367488 | tf_op jit(solution)/shard_map/while/body/eval_jaxpr/scatter-add | solution.py:76
  605.9 6.2 gather_fusion
  618.4 12.6 %scatter_fusion = f32[3585,96]{1,0:T(8,128)S(1)} fusion(f32[3585,96]{1,0:T(8,128)S(1)} %get-tuple-element.299, s32[2048]{0:T(1024)S(1)} %bitcast.61, f32[2048,96]{1,0:T(8,128)} %copy.43), kind=kCustom, calls=%fused_computation.3.clone.clone.1 | custom fusion | flops 196608 | bytes 2367488 | tf_op jit(solution)/shard_map/while/body/eval_jaxpr/scatter-add | solution.py:76
  631.9 6.2 gather_fusion
  644.4 12.6 %scatter_fusion = f32[3585,96]{1,0:T(8,128)S(1)} fusion(f32[3585,96]{1,0:T(8,128)S(1)} %get-tuple-element.299, s32[2048]{0:T(1024)S(1)} %bitcast.61, f32[2048,96]{1,0:T(8,128)} %copy.43), kind=kCustom, calls=%fused_computation.3.clone.clone.1 | custom fusion | flops 196608 | bytes 2367488 | tf_op jit(solution)/shard_map/while/body/eval_jaxpr/scatter-add | solution.py:76
  657.9 6.2 gather_fusion
  670.4 12.6 %scatter_fusion = f32[3585,96]{1,0:T(8,128)S(1)} fusion(f32[3585,96]{1,0:T(8,128)S(1)} %get-tuple-element.299, s32[2048]{0:T(1024)S(1)} %bitcast.61, f32[2048,96]{1,0:T(8,128)} %copy.43), kind=kCustom, calls=%fused_computation.3.clone.clone.1 | custom fusion | flops 196608 | bytes 2367488 | tf_op jit(solution)/shard_map/while/body/eval_jaxpr/scatter-add | solution.py:76
  683.9 6.2 gather_fusion
  696.4 12.6 %scatter_fusion = f32[3585,96]{1,0:T(8,128)S(1)} fusion(f32[3585,96]{1,0:T(8,128)S(1)} %get-tuple-element.299, s32[2048]{0:T(1024)S(1)} %bitcast.61, f32[2048,96]{1,0:T(8,128)} %copy.43), kind=kCustom, calls=%fused_computation.3.clone.clone.1 | custom fusion | flops 196608 | bytes 2367488 | tf_op jit(solution)/shard_map/while/body/eval_jaxpr/scatter-add | solution.py:76
  709.9 6.2 gather_fusion
  722.4 12.6 %scatter_fusion = f32[3585,96]{1,0:T(8,128)S(1)} fusion(f32[3585,96]{1,0:T(8,128)S(1)} %get-tuple-element.299, s32[2048]{0:T(1024)S(1)} %bitcast.61, f32[2048,96]{1,0:T(8,128)} %copy.43), kind=kCustom, calls=%fused_computation.3.clone.clone.1 | custom fusion | flops 196608 | bytes 2367488 | tf_op jit(solution)/shard_map/while/body/eval_jaxpr/scatter-add | solution.py:76
  738.6 22.6 %all-to-all-start.1 = ((bf16[4,256,96]{1,2,0:T(8,128)(2,1)}), bf16[4,256,96]{1,2,0:T(8,128)(2,1)S(1)}, u32[]{:S(2)}, u32[]{:S(2)}) async-start(bf16[4,256,96]{1,2,0:T(8,128)(2,1)} %copy.33), calls=%async_computation.1 | async-start | bytes 393216 | tf_op jit(solution)/shard_map/all_to_all | solution.py:98
  764.8 7.0 scatter_fusion.1
  771.8 17.6 %collective-permute-start.2 = (bf16[256,96]{1,0:T(8,128)(2,1)S(1)}, bf16[256,96]{1,0:T(8,128)(2,1)S(1)}, u32[]{:S(2)}, u32[]{:S(2)}) collective-permute-start(bf16[256,96]{1,0:T(8,128)(2,1)S(1)} %get-tuple-element.221), channel_id=1, source_target_pairs={{0,1},{1,2},{2,3},{4,5},{5,6},{6,7},{8,9},{9,10},{10,11},{12,13},{... | collective-permute-start | bytes 147464 | tf_op jit(solution)/shard_map/ppermute | solution.py:14
  789.5 4.0 collective-permute-start.3
  795.1 4.0 scatter_custom_fusion.2
  800.4 73.4 %all-reduce.3.cloned.1.call-done = f32[96,2592]{0,1:T(8,128)} async-done(((f32[96,2592]{0,1:T(8,128)}), f32[96,2592]{0,1:T(8,128)}) %all-reduce.3.cloned.1.call-update) | async-done | bytes 995344 | tf_op jit(solution)/shard_map/psum | solution.py:93
  (364 shorter events, 220.1 us)
Async XLA Ops:
  9.9 7.2 copy-start.7
  11.5 6.9 collective-permute-start
  15.2 5.6 collective-permute-start.1
  17.1 7.0 copy-start.5
  24.1 5.6 copy-start.3
  25.0 8.1 all-to-all-start
  40.5 3.5 copy-start.2
  66.1 2.7 copy-start.4
  66.1 3.9 copy-start.2
  92.1 2.7 copy-start.4
  92.1 3.9 copy-start.2
  118.1 2.7 copy-start.4
  118.1 3.9 copy-start.2
  144.1 2.7 copy-start.4
  144.1 3.9 copy-start.2
  170.1 2.7 copy-start.4
  170.1 3.9 copy-start.2
  196.1 2.7 copy-start.4
  196.1 3.9 copy-start.2
  222.1 2.7 copy-start.4
  222.1 3.9 copy-start.2
  248.1 2.7 copy-start.4
  248.1 3.9 copy-start.2
  274.1 2.7 copy-start.4
  274.1 3.9 copy-start.2
  300.1 2.7 copy-start.4
  300.1 3.9 copy-start.2
  326.1 3.9 copy-start.2
  352.1 2.7 copy-start.4
  352.1 3.9 copy-start.2
  378.1 2.7 copy-start.4
  378.1 3.9 copy-start.2
  404.1 2.7 copy-start.4
  404.1 3.9 copy-start.2
  430.1 2.7 copy-start.4
  430.1 3.9 copy-start.2
  456.1 3.9 copy-start.2
  482.1 3.9 copy-start.2
  508.1 2.7 copy-start.4
  508.1 3.9 copy-start.2
  534.1 2.7 copy-start.4
  534.1 3.9 copy-start.2
  560.1 2.7 copy-start.4
  560.1 3.9 copy-start.2
  586.1 2.7 copy-start.4
  586.1 3.9 copy-start.2
  612.1 2.7 copy-start.4
  612.1 3.9 copy-start.2
  638.1 2.7 copy-start.4
  638.1 3.9 copy-start.2
  664.1 2.7 copy-start.4
  664.1 3.9 copy-start.2
  690.1 2.7 copy-start.4
  690.1 3.9 copy-start.2
  716.1 2.7 copy-start.4
  716.1 3.9 copy-start.2
  737.8 24.2 %copy-start.1 = (f32[2048,96]{0,1:T(8,128)S(1)}, f32[2048,96]{0,1:T(8,128)}, u32[]{:S(2)}) copy-start(f32[2048,96]{0,1:T(8,128)} %get-tuple-element.159) | copy-start | bytes 2359300
  738.6 26.0 %all-to-all-start.1 = ((bf16[4,256,96]{1,2,0:T(8,128)(2,1)}), bf16[4,256,96]{1,2,0:T(8,128)(2,1)S(1)}, u32[]{:S(2)}, u32[]{:S(2)}) async-start(bf16[4,256,96]{1,2,0:T(8,128)(2,1)} %copy.33), calls=%async_computation.1 | async-start | bytes 393216 | tf_op jit(solution)/shard_map/all_to_all | solution.py:98
  761.2 112.6 %all-reduce.3.cloned.1.call-start = ((), (), s32[]{:S(2)}) async-start(), calls=%async_computation.2 | async-start | bytes 2654208 | tf_op jit(solution)/shard_map/psum | solution.py:93
  761.2 3.5 copy-start
  761.2 3.5 copy-start.6
  771.7 21.7 %copy-start.9 = (pred[2049]{0:T(1024)(128)(4,1)S(1)}, pred[2049]{0:T(1024)(128)(4,1)}, u32[]{:S(2)}) copy-start(pred[2049]{0:T(1024)(128)(4,1)} %constant.114.clone.1) | copy-start | bytes 6151
  771.8 22.0 %collective-permute-start.2 = (bf16[256,96]{1,0:T(8,128)(2,1)S(1)}, bf16[256,96]{1,0:T(8,128)(2,1)S(1)}, u32[]{:S(2)}, u32[]{:S(2)}) collective-permute-start(bf16[256,96]{1,0:T(8,128)(2,1)S(1)} %get-tuple-element.221), channel_id=1, source_target_pairs={{0,1},{1,2},{2,3},{4,5},{5,6},{6,7},{8,9},{9,10},{10,11},{12,13},{... | collective-permute-start | bytes 147464 | tf_op jit(solution)/shard_map/ppermute | solution.py:14
  789.5 5.6 collective-permute-start.3
  (5 other events, 11.1 us)
Sparse Core Ops, SparseCore 0:
  765.5 108.2 all-reduce.2
where the time goes:
time: 894 us; the launch traced here: 883 us
  other arithmetic  383 us (43%)
  local copies, waits for them, and re-layouts  214 us (24%)
  matrix products  133 us (15%)
  waiting for transfers between devices  81.9 us (9%)
  starting transfers between devices  54.5 us (6%)
  between operations  14.4 us (2%)
    scatter-add x27, other arithmetic, offset_step(): grad_padded = grad_padded.at[safe_index].add(back_grad)  340 us
    gather x27, local copies, waits for them, and re-layouts, offset_step(): gathered = jnp.take(padded_table, safe_index, axis=0)  167 us
    psum x1, waiting for transfers between devices, on_device(): w_total = lax.psum(w_term, ('xy', 'gz'))  73.4 us
    dot_general x27, matrix products, offset_step(): jnp.dot(gathered, w_offset, preferred_element_type=jnp.float32)  71.7 us
    dot_general x27, local copies, waits for them, and re-layouts, offset_step(): lax.dot_general(upstream_rows, w_offset, (((1,), (1,)), ((), ())), prefer...  35.5 us
    dot_general x27, matrix products, offset_step(): w_piece = jnp.dot(cotangent, gathered, preferred_element_type=jnp.float32)  33.4 us
    dot_general x27, matrix products, offset_step(): lax.dot_general(upstream_rows, w_offset, (((1,), (1,)), ((), ())), prefer...  28.1 us
    select_n x27, other arithmetic, offset_step(): gathered = jnp.take(padded_table, safe_index, axis=0)  23.3 us
  transfers between devices with their start and end apart: 7, of which 5 were waited for; matrix products, arithmetic and copies ran while one was open for 2% of the time, Pallas kernels for 0%

commit v1 on v0

v1 whole, which is shorter than its diff:
```python
import functools
import math

import jax
import jax.numpy as jnp
from jax import lax
from jax.experimental import pallas as pl
from jax.experimental.pallas import tpu as pltpu
from jax.sharding import PartitionSpec as P

LO = 256
BF = jnp.bfloat16
F32 = jnp.float32
VMEM_LIMIT = 56 * 1024 * 1024


def split_index(index):
    return index >> 8, index & (LO - 1)


def one_hot(lo):
    rows = lax.broadcasted_iota(jnp.int32, (LO, lo.shape[1]), 0)
    return jnp.where(rows == lo, 1.0, 0.0).astype(BF)


def pick(blocks, index):
    count, channels, _ = blocks.shape
    hi, lo = split_index(index)
    found = jnp.dot(
        blocks.reshape(count * channels, LO), one_hot(lo), preferred_element_type=F32
    ).reshape(count, channels, index.shape[1])
    got = jnp.zeros((channels, index.shape[1]), F32)
    for h in range(count):
        got = jnp.where(hi == h, found[h], got)
    return got.astype(BF)


def spread(values, index, first, count):
    channels, width = values.shape
    hi, lo = split_index(index)
    parts = [values * jnp.where(hi == first + h, 1.0, 0.0).astype(BF) for h in range(count)]
    wide = jnp.concatenate(parts, axis=0)
    added = lax.dot_general(
        wide, one_hot(lo), (((1,), (1,)), ((), ())), preferred_element_type=F32
    )
    return added.reshape(count, channels, LO)


def whole(array_or_shape):
    shape = array_or_shape.shape
    return pl.BlockSpec(shape, lambda *_: (0,) * len(shape))


def params():
    return pltpu.CompilerParams(vmem_limit_bytes=VMEM_LIMIT)


def fill_blocks(blocks, own_ref, *rest):
    count = own_ref.shape[1] // LO
    for h in range(count):
        blocks[h] = own_ref[:, h * LO : (h + 1) * LO]
    at = count
    for ref in rest:
        blocks[at : at + ref.shape[0]] = ref[...]
        at += ref.shape[0]


def pick_kernel(*refs):
    index_ref, out_ref, blocks = refs[-3], refs[-2], refs[-1]
    fill_blocks(blocks, *refs[:-3])
    for b in range(out_ref.shape[0]):
        out_ref[b] = pick(blocks[...], index_ref[:, b * LO : (b + 1) * LO])


def pick_blocks(own, rest, index):
    channels, slots = own.shape
    width = index.shape[0]
    count = slots // LO + sum(r.shape[0] for r in rest)
    return pl.pallas_call(
        pick_kernel,
        out_shape=jax.ShapeDtypeStruct((width // LO, channels, LO), BF),
        scratch_shapes=[pltpu.VMEM((count, channels, LO), BF)],
        compiler_params=params(),
        name="pick_columns",
    )(own, *rest, index.reshape(1, width))


def conv_kernel(chunk, own_ref, z_ref, xy_ref, wt_ref, index_ref, up_ref, out_ref, wg_ref, blocks, got):
    k = pl.program_id(0)
    channels, slots = own_ref.shape

    @pl.when(k == 0)
    def _():
        fill_blocks(blocks, own_ref, z_ref, xy_ref)

    rows = pl.ds(pl.multiple_of(k * channels, 32), channels)

    @pl.loop(0, slots // chunk)
    def _(j):
        cols = pl.ds(pl.multiple_of(j * chunk, chunk), chunk)
        got[rows, cols] = pick(blocks[...], index_ref[0, :, cols])

    @pl.when(k == pl.num_programs(0) - 1)
    def _():
        @pl.loop(0, slots // LO)
        def _(j):
            cols = pl.ds(pl.multiple_of(j * LO, LO), LO)
            out_ref[:, cols] = jnp.dot(
                wt_ref[...], got[:, cols], preferred_element_type=F32
            ).astype(BF)

        @pl.loop(0, got.shape[0] // (3 * channels))
        def _(j):
            part = pl.ds(pl.multiple_of(j * 3 * channels, 32), 3 * channels)
            wg_ref[part, :] = lax.dot_general(
                got[part, :], up_ref[...], (((1,), (1,)), ((), ())), preferred_element_type=F32
            )


def convolve(own, z_blocks, xy_blocks, weight_t, index, up, chunk=512):
    channels, slots = own.shape
    offsets = index.shape[0]
    count = slots // LO + z_blocks.shape[0] + xy_blocks.shape[0]
    flops = 2 * offsets * slots * channels * (count * LO + 2 * channels)
    return pl.pallas_call(
        functools.partial(conv_kernel, chunk),
        grid=(offsets,),
        in_specs=[
            whole(own),
            whole(z_blocks),
            whole(xy_blocks),
            whole(weight_t),
            pl.BlockSpec((1, 1, slots), lambda k: (k, 0, 0)),
            whole(up),
        ],
        out_specs=[
            pl.BlockSpec((channels, slots), lambda k: (0, 0)),
            pl.BlockSpec((offsets * channels, channels), lambda k: (0, 0)),
        ],
        out_shape=[
            jax.ShapeDtypeStruct((channels, slots), BF),
            jax.ShapeDtypeStruct((offsets * channels, channels), F32),
        ],
        scratch_shapes=[
            pltpu.VMEM((count, channels, LO), BF),
            pltpu.VMEM((offsets * channels, slots), BF),
        ],
        compiler_params=params(),
        cost_estimate=pl.CostEstimate(flops=flops, bytes_accessed=4 << 20, transcendentals=0),
        name="convolve",
    )(own, z_blocks, xy_blocks, weight_t, index, up)


def spread_kernel(first, chunk, w_ref, index_ref, up_ref, acc_ref):
    @pl.when(pl.program_id(0) == 0)
    def _():
        acc_ref[...] = jnp.zeros_like(acc_ref)

    @pl.loop(0, up_ref.shape[1] // chunk)
    def _(j):
        cols = pl.ds(pl.multiple_of(j * chunk, chunk), chunk)
        back = jnp.dot(w_ref[0], up_ref[:, cols], preferred_element_type=F32).astype(BF)
        acc_ref[...] += spread(back, index_ref[0, :, cols], first, acc_ref.shape[0])


def spread_grads(weight, index, up, first, count, chunk=1024):
    channels, slots = up.shape
    offsets = index.shape[0]
    flops = 2 * offsets * slots * channels * (count * LO + channels)
    return pl.pallas_call(
        functools.partial(spread_kernel, first, chunk),
        grid=(offsets,),
        in_specs=[
            pl.BlockSpec((1, channels, channels), lambda k: (k, 0, 0)),
            pl.BlockSpec((1, 1, slots), lambda k: (k, 0, 0)),
            whole(up),
        ],
        out_specs=pl.BlockSpec((count, channels, LO), lambda k: (0, 0, 0)),
        out_shape=jax.ShapeDtypeStruct((count, channels, LO), F32),
        compiler_params=params(),
        cost_estimate=pl.CostEstimate(flops=flops, bytes_accessed=2 << 20, transcendentals=0),
        name="spread_grads",
    )(weight, index, up)


def add_kernel(blocks_ref, index_ref, out_ref):
    for b in range(blocks_ref.shape[0]):
        part = spread(blocks_ref[b], index_ref[:, b * LO : (b + 1) * LO], 0, out_ref.shape[0])
        if b == 0:
            out_ref[...] = part
        else:
            out_ref[...] += part


def add_blocks(blocks, index, count):
    _, channels, _ = blocks.shape
    return pl.pallas_call(
        add_kernel,
        out_shape=jax.ShapeDtypeStruct((count, channels, LO), F32),
        compiler_params=params(),
        name="add_columns",
    )(blocks, index.reshape(1, -1))


def last_kernel(own_ref, ext_ref, blocks_ref, index_ref, out_ref):
    count = own_ref.shape[0]
    total = own_ref[...] + ext_ref[...]
    for b in range(blocks_ref.shape[0]):
        total += spread(blocks_ref[b], index_ref[:, b * LO : (b + 1) * LO], 0, count)
    for h in range(count):
        out_ref[:, h * LO : (h + 1) * LO] = total[h]


def last_add(own, ext, blocks, index):
    count, channels, _ = own.shape
    return pl.pallas_call(
        last_kernel,
        grid=(1,),
        in_specs=[
            whole(own),
            pl.BlockSpec(own.shape, lambda i: (0, 0, 0)),
            whole(blocks),
            pl.BlockSpec((1, index.shape[0]), lambda i: (0, 0)),
        ],
        out_specs=pl.BlockSpec((channels, count * LO), lambda i: (0, 0)),
        out_shape=jax.ShapeDtypeStruct((channels, count * LO), F32),
        compiler_params=params(),
        name="last_add",
    )(own, ext, blocks, index.reshape(1, -1))


def exchange(blocks, peers, per_peer):
    count, channels, _ = blocks.shape
    if per_peer != LO:
        flat = blocks.transpose(1, 0, 2).reshape(channels, peers, per_peer).transpose(1, 0, 2)
    else:
        flat = blocks
    got = lax.all_to_all(flat, "xy", split_axis=0, concat_axis=0, tiled=True)
    if per_peer != LO:
        got = got.transpose(1, 0, 2).reshape(channels, count, LO).transpose(1, 0, 2)
    return got


def shift_z(low_bound, high_bound):
    count = lax.axis_size("gz")
    up = [(i, i + 1) for i in range(count - 1)]
    down = [(b, a) for a, b in up]
    return lax.ppermute(high_bound, "gz", up), lax.ppermute(low_bound, "gz", down)


def on_device(features, weight, z_send, xy_send, kernel_map, cotangent):
    channels, slots = features.shape
    offsets = weight.shape[0]
    peers = lax.axis_size("xy")
    z_list, xy_list = z_send.reshape(-1), xy_send.reshape(-1)
    z_count = z_list.shape[0] // LO
    rim = z_count // 2
    xy_count = xy_list.shape[0] // LO
    per_peer = xy_list.shape[0] // peers
    own_count = slots // LO
    ext_count = own_count + z_count
    index = kernel_map.reshape(offsets, 1, slots)

    outgoing = pick_blocks(features, (), z_list)
    below, above = shift_z(outgoing[:rim], outgoing[rim:])
    z_blocks = jnp.concatenate([below, above], axis=0)

    halo_grad = spread_grads(weight, index, cotangent, own_count, z_count + xy_count)

    sends = pick_blocks(features, (z_blocks,), xy_list)
    xy_blocks = exchange(sends, peers, per_peer)
    returned = exchange(halo_grad[z_count:].astype(BF), peers, per_peer)
    ext_grad = add_blocks(returned, xy_list, ext_count)
    z_grad = (halo_grad[:z_count] + ext_grad[own_count:]).astype(BF)
    back_low, back_high = shift_z(z_grad[:rim], z_grad[rim:])
    z_back = jnp.concatenate([back_low, back_high], axis=0)

    weight_t = weight.transpose(2, 0, 1).reshape(channels, offsets * channels)
    out_features, w_term = convolve(features, z_blocks, xy_blocks, weight_t, index, cotangent)
    w_scale = 1.0 / math.sqrt(slots * peers * lax.axis_size("gz"))
    w_mine = lax.psum_scatter(w_term.T, "xy", scatter_dimension=0, tiled=True)
    grad_weight = lax.psum(w_mine, "gz") * w_scale

    own_grad = spread_grads(weight, index, cotangent, 0, own_count)
    grad_features = last_add(own_grad, ext_grad, z_back, z_list)
    return (out_features, grad_features, grad_weight)


def solution(mesh):
    slab = P(None, ("parts", "xy", "gz"))
    lists = P(("parts", "xy"), "gz", None)
    return jax.shard_map(
        on_device,
        mesh=mesh,
        in_specs=(slab, P(), lists, lists, slab, slab),
        out_specs=(slab, slab, P(("parts", "xy"), None)),
        check_vma=False,
    )
```

time: 894 us -> 224 us (0.25)
  other arithmetic: 383 us -> 3.14 us
  local copies, waits for them, and re-layouts: 214 us -> 10.9 us
  Pallas kernels: 0 us -> 154 us
  matrix products: 133 us -> 0 us
  waiting for transfers between devices: 81.9 us -> 16.8 us
  starting transfers between devices: 54.5 us -> 20.5 us
    scatter-add x29 -> x0, other arithmetic: 351 us -> none  [the longest x27 340 us: offset_step(): grad_padded = grad_padded.at[safe_index].add(back_grad)]
    gather x30 -> x0, local copies, waits for them, and re-layouts: 172 us -> none  [the longest x27 167 us: offset_step(): gathered = jnp.take(padded_table, safe_index, axis=0)]
    pallas_call x0 -> x7, Pallas kernels: none -> 154 us  [the longest x2 76.1 us: spread_grads(): pl.pallas_call(functools.partial(spread_kernel, first, chunk), grid=(offs...]
    dot_general x81 -> x0, matrix products: 133 us -> none  [the longest x27 71.7 us: offset_step(): jnp.dot(gathered, w_offset, preferred_element_type=jnp.float32)]
    psum x1, waiting for transfers between devices: 73.4 us -> 0.01 us  [on_device(): grad_weight = lax.psum(w_mine, 'gz') * w_scale]
    dot_general x27 -> x0, local copies, waits for them, and re-layouts: 35.5 us -> none  [offset_step(): lax.dot_general(upstream_rows, w_offset, (((1,), (1,)), ((), ())), prefer...]
    select_n x31 -> x0, other arithmetic: 24.9 us -> none  [the longest x27 23.3 us: offset_step(): gathered = jnp.take(padded_table, safe_index, axis=0)]
    ppermute x4, starting transfers between devices: 27.2 us -> 9.91 us  [the longest x2 5.59 us: shift_z(): lax.ppermute(high_bound, 'gz', up)]
  transfers between devices with their start and end apart: 7 -> 8, of which waited for: 5 -> 4; matrix products, arithmetic and copies ran while one was open for 2% -> 4% of each run, Pallas kernels for 0% -> 37%
where the time goes in v1:
time: 224 us; the launch traced here: 220 us
  Pallas kernels  154 us (69%)
  starting transfers between devices  20.5 us (9%)
  waiting for transfers between devices  16.8 us (8%)
  between operations  14.7 us (7%)
  local copies, waits for them, and re-layouts  10.9 us (5%)
  other arithmetic  3.14 us (1%)
    pallas_call x2, Pallas kernels, spread_grads(): pl.pallas_call(functools.partial(spread_kernel, first, chunk), grid=(offs...  76.1 us
    pallas_call x1, Pallas kernels, convolve(): pl.pallas_call(functools.partial(conv_kernel, chunk), grid=(offsets,), in...  68.3 us
    all_to_all x2, starting transfers between devices, exchange(): got = lax.all_to_all(flat, 'xy', split_axis=0, concat_axis=0, tiled=True)  10.6 us
    all_to_all x2, waiting for transfers between devices, exchange(): got = lax.all_to_all(flat, 'xy', split_axis=0, concat_axis=0, tiled=True)  10.2 us
    unnamed x16, local copies, waits for them, and re-layouts  6.5 us
    ppermute x2, starting transfers between devices, shift_z(): lax.ppermute(high_bound, 'gz', up)  5.59 us
    pallas_call x2, Pallas kernels, pick_blocks(): pl.pallas_call(pick_kernel, out_shape=jax.ShapeDtypeStruct((width // LO,...  4.51 us
  transfers between devices with their start and end apart: 8, of which 4 were waited for; matrix products, arithmetic and copies ran while one was open for 4% of the time, Pallas kernels for 37%

profile of v1, /device:TPU:17, one launch (start us, length us, event | category | flops | bytes accessed | tf_op | source)
XLA Modules:
  0.0 220.3 jit_solution(16658127044246225030)
XLA Ops:
  7.2 0.0 copy-start.2
  7.2 0.0 copy-start.1
  7.2 2.1 pick_columns.2
  9.3 0.8 fusion.2
  10.1 3.7 %collective-permute-start = (bf16[1,96,256]{2,1,0:T(8,128)(2,1)S(1)}, bf16[1,96,256]{2,1,0:T(8,128)(2,1)S(1)}, u32[]{:S(2)}, u32[]{:S(2)}) collective-permute-start(bf16[1,96,256]{2,1,0:T(8,128)(2,1)S(1)} %get-tuple-element.19), channel_id=1, source_target_pairs={{0,1},{1,2},{2,3},{4,5},{5,6},{6,7},{8,9},{9,10},{10,11},{12,13},{... | collective-permute-start | bytes 147464 | tf_op jit(solution)/shard_map/ppermute | solution.py:248
  13.8 1.9 collective-permute-start.1
  15.7 0.0 collective-permute-done
  15.7 3.5 %collective-permute-done.1 = bf16[1,96,256]{2,1,0:T(8,128)(2,1)S(1)} collective-permute-done((bf16[1,96,256]{2,1,0:T(8,128)(2,1)S(1)}, bf16[1,96,256]{2,1,0:T(8,128)(2,1)S(1)}, u32[]{:S(2)}, u32[]{:S(2)}) %collective-permute-start.1) | collective-permute-done | bytes 49184 | tf_op jit(solution)/shard_map/ppermute | solution.py:248
  19.2 0.0 copy-start.3
  19.2 0.6 copy-done.3
  19.8 2.4 %pick_columns.3 = bf16[4,96,256]{2,1,0:T(8,128)(2,1)} custom-call(bf16[96,2048]{1,0:T(8,128)(2,1)} %own_ref.1, bf16[2,96,256]{2,1,0:T(8,128)(2,1)} %copy-done.3, s32[1,1024]{1,0:T(1,128)} %bitcast.11), custom_call_target="tpu_custom_call" | custom-call | tf_op jit(solution)/shard_map/pick_columns/pallas_call | solution.py:79
  22.2 4.6 %all-to-all-start = ((bf16[4,96,256]{2,1,0:T(8,128)(2,1)}), bf16[4,96,256]{2,1,0:T(8,128)(2,1)S(1)}, u32[]{:S(2)}, u32[]{:S(2)}) async-start(bf16[4,96,256]{2,1,0:T(8,128)(2,1)} %pick_columns.3), calls=%async_computation | async-start | bytes 393216 | tf_op jit(solution)/shard_map/all_to_all | solution.py:238
  26.9 0.0 all-reduce.6.cloned.1.call-start
  26.9 0.0 copy-done.2
  26.9 0.8 reshape.13.index_ref
  27.7 0.0 copy-done.1
  27.7 1.1 copy.13.wt_ref
  28.8 1.7 all-to-all-done.xy_ref
  30.5 0.0 copy-start.4
  30.5 0.7 copy-done.4
  31.1 68.3 %convolve.1 = (bf16[96,2048]{1,0:T(8,128)(2,1)}, f32[2592,96]{1,0:T(8,128)}) custom-call(bf16[96,2048]{1,0:T(8,128)(2,1)} %own_ref.1, bf16[2,96,256]{2,1,0:T(8,128)(2,1)} %copy-done.3, bf16[4,96,256]{2,1,0:T(8,128)(2,1)} %copy-done.4, bf16[96,2592]{1,0:T(8,128)(2,1)} %copy.13.wt_ref, s32[27,1,2048]{2,1,0:T(1,128)} %reshape.13.index_ref, bf16[96,2048]{1,0:T(8,128)(2,1)} %up_ref.5), custom_call_target="tpu_custom_call" | custom-call | flops 40089157632 | bytes 4194304 | tf_op jit(solution)/shard_map/convolve/pallas_call | solution.py:125
  99.4 0.0 all-reduce.6.cloned.1.call-update
  99.4 0.0 copy-start.5
  99.5 35.3 %spread_grads.3 = f32[6,96,256]{2,1,0:T(8,128)} custom-call(bf16[27,96,96]{2,1,0:T(8,128)(2,1)} %w_ref.3, s32[27,1,2048]{2,1,0:T(1,128)} %reshape.13.index_ref, bf16[96,2048]{1,0:T(8,128)(2,1)} %up_ref.5), custom_call_target="tpu_custom_call" | custom-call | flops 17326669824 | bytes 2097152 | tf_op jit(solution)/shard_map/spread_grads/pallas_call | solution.py:170
  134.8 1.7 slice.41
  136.5 6.0 %all-to-all-start.1 = ((bf16[4,96,256]{2,1,0:T(8,128)(2,1)}), bf16[4,96,256]{2,1,0:T(8,128)(2,1)S(1)}, u32[]{:S(2)}, u32[]{:S(2)}) async-start(bf16[4,96,256]{2,1,0:T(8,128)(2,1)} %slice.41), calls=%async_computation.1 | async-start | bytes 393216 | tf_op jit(solution)/shard_map/all_to_all | solution.py:238
  142.4 0.0 all-reduce.4.cloned.1.call-start
  142.4 0.0 copy-done.5
  142.4 0.5 dynamic-slice
  143.5 8.5 %all-to-all-done.1.blocks_ref = bf16[4,96,256]{2,1,0:T(8,128)(2,1)S(1)} async-done(((bf16[4,96,256]{2,1,0:T(8,128)(2,1)}), bf16[4,96,256]{2,1,0:T(8,128)(2,1)S(1)}, u32[]{:S(2)}, u32[]{:S(2)}) %all-to-all-start.1) | async-done | bytes 196640 | tf_op jit(solution)/shard_map/all_to_all | solution.py:238
  152.1 0.0 copy-start
  152.1 0.7 copy-done
  152.7 2.6 %add_columns.1.ext_ref = f32[10,96,256]{2,1,0:T(8,128)} custom-call(bf16[4,96,256]{2,1,0:T(8,128)(2,1)} %copy-done, s32[1,1024]{1,0:T(1,128)} %bitcast.12), custom_call_target="tpu_custom_call" | custom-call | tf_op jit(solution)/shard_map/add_columns/pallas_call | solution.py:197
  155.3 1.1 fusion
  156.4 1.9 collective-permute-start.2
  158.3 2.4 %collective-permute-start.3 = (bf16[1,96,256]{2,1,0:T(8,128)(2,1)S(1)}, bf16[1,96,256]{2,1,0:T(8,128)(2,1)S(1)}, u32[]{:S(2)}, u32[]{:S(2)}) collective-permute-start(bf16[1,96,256]{2,1,0:T(8,128)(2,1)S(1)} %get-tuple-element.17), channel_id=1, source_target_pairs={{1,0},{2,1},{3,2},{5,4},{6,5},{7,6},{9,8},{10,9},{11,10},{13,12},{... | collective-permute-start | bytes 147464 | tf_op jit(solution)/shard_map/ppermute | solution.py:248
  160.7 3.1 %all-reduce.6.cloned.1.call-done = f32[96,2592]{0,1:T(8,128)} async-done(((f32[96,2592]{0,1:T(8,128)}), f32[96,2592]{0,1:T(8,128)}) %all-reduce.6.cloned.1.call-update) | async-done | bytes 995344
  163.9 2.8 %constant_dynamic-slice_fusion = f32[24,2592]{0,1:T(8,128)} fusion(f32[96,2592]{0,1:T(8,128)} %all-reduce.6.cloned.1.call-done, u32[]{:T(128)S(6)} %multiply.1), kind=kLoop, calls=%fused_computation.7 | loop fusion | bytes 497668
  166.7 0.0 all-reduce.4.cloned.1.call-update
  166.7 40.8 %spread_grads.2.own_ref = f32[8,96,256]{2,1,0:T(8,128)} custom-call(bf16[27,96,96]{2,1,0:T(8,128)(2,1)} %w_ref.3, s32[27,1,2048]{2,1,0:T(1,128)} %reshape.13.index_ref, bf16[96,2048]{1,0:T(8,128)(2,1)} %up_ref.5), custom_call_target="tpu_custom_call" | custom-call | flops 22762487808 | bytes 2097152 | tf_op jit(solution)/shard_map/spread_grads/pallas_call | solution.py:170
  207.6 0.0 collective-permute-done.2
  207.6 0.0 collective-permute-done.3
  207.6 0.7 pad_maximum_fusion.blocks_ref
  208.2 2.7 %last_add.1 = f32[96,2048]{1,0:T(8,128)} custom-call(f32[8,96,256]{2,1,0:T(8,128)} %spread_grads.2.own_ref, f32[10,96,256]{2,1,0:T(8,128)} %add_columns.1.ext_ref, bf16[2,96,256]{2,1,0:T(8,128)(2,1)} %pad_maximum_fusion.blocks_ref, s32[1,512]{1,0:T(1,128)} %bitcast.14), custom_call_target="tpu_custom_call" | custom-call | tf_op jit(solution)/shard_map/last_add/pallas_call | solution.py:216
  210.9 0.0 all-reduce.4.cloned.1.call-done
  210.9 1.4 broadcast_multiply_fusion
  212.3 1.1 copy.14
  (3 shorter events, 0.0 us)
Async XLA Ops:
  7.2 19.7 %copy-start.2 = (s32[27,2048]{1,0:T(8,128)S(1)}, s32[27,2048]{1,0:T(8,128)}, u32[]{:S(2)}) copy-start(s32[27,2048]{1,0:T(8,128)} %param.10) | copy-start | bytes 663556
  7.2 20.6 %copy-start.1 = (bf16[27,96,96]{2,1,0:T(8,128)(2,1)S(1)}, bf16[27,96,96]{2,1,0:T(8,128)(2,1)}, u32[]{:S(2)}) copy-start(bf16[27,96,96]{2,1,0:T(8,128)(2,1)} %w_ref.3) | copy-start | bytes 1492996
  10.1 5.6 %collective-permute-start = (bf16[1,96,256]{2,1,0:T(8,128)(2,1)S(1)}, bf16[1,96,256]{2,1,0:T(8,128)(2,1)S(1)}, u32[]{:S(2)}, u32[]{:S(2)}) collective-permute-start(bf16[1,96,256]{2,1,0:T(8,128)(2,1)S(1)} %get-tuple-element.19), channel_id=1, source_target_pairs={{0,1},{1,2},{2,3},{4,5},{5,6},{6,7},{8,9},{9,10},{10,11},{12,13},{... | collective-permute-start | bytes 147464 | tf_op jit(solution)/shard_map/ppermute | solution.py:248
  13.8 5.4 %collective-permute-start.1 = (bf16[1,96,256]{2,1,0:T(8,128)(2,1)S(1)}, bf16[1,96,256]{2,1,0:T(8,128)(2,1)S(1)}, u32[]{:S(2)}, u32[]{:S(2)}) collective-permute-start(bf16[1,96,256]{2,1,0:T(8,128)(2,1)S(1)} %get-tuple-element.18), channel_id=1, source_target_pairs={{1,0},{2,1},{3,2},{5,4},{6,5},{7,6},{9,8},{10,9},{11,10},{13,12},{... | collective-permute-start | bytes 147464 | tf_op jit(solution)/shard_map/ppermute | solution.py:248
  19.2 0.6 copy-start.3
  22.2 8.2 %all-to-all-start = ((bf16[4,96,256]{2,1,0:T(8,128)(2,1)}), bf16[4,96,256]{2,1,0:T(8,128)(2,1)S(1)}, u32[]{:S(2)}, u32[]{:S(2)}) async-start(bf16[4,96,256]{2,1,0:T(8,128)(2,1)} %pick_columns.3), calls=%async_computation | async-start | bytes 393216 | tf_op jit(solution)/shard_map/all_to_all | solution.py:238
  26.9 137.0 %all-reduce.6.cloned.1.call-start = ((), (), s32[]{:S(2)}) async-start(), calls=%async_computation.3 | async-start | bytes 2654208
  30.5 0.7 copy-start.4
  99.4 43.0 %copy-start.5 = (u32[32]{0:T(128)S(1)}, u32[32]{0:T(128)}, u32[]{:S(2)}) copy-start(u32[32]{0:T(128)} %constant.6) | copy-start | bytes 388
  136.5 15.6 %all-to-all-start.1 = ((bf16[4,96,256]{2,1,0:T(8,128)(2,1)}), bf16[4,96,256]{2,1,0:T(8,128)(2,1)S(1)}, u32[]{:S(2)}, u32[]{:S(2)}) async-start(bf16[4,96,256]{2,1,0:T(8,128)(2,1)} %slice.41), calls=%async_computation.1 | async-start | bytes 393216 | tf_op jit(solution)/shard_map/all_to_all | solution.py:238
  142.4 68.5 %all-reduce.4.cloned.1.call-start = ((), (), s32[]{:S(2)}) async-start(), calls=%async_computation.2 | async-start | bytes 2654208 | tf_op jit(solution)/shard_map/psum | solution.py:282
  152.1 0.7 copy-start
  156.4 51.2 %collective-permute-start.2 = (bf16[1,96,256]{2,1,0:T(8,128)(2,1)S(1)}, bf16[1,96,256]{2,1,0:T(8,128)(2,1)S(1)}, u32[]{:S(2)}, u32[]{:S(2)}) collective-permute-start(bf16[1,96,256]{2,1,0:T(8,128)(2,1)S(1)} %get-tuple-element.16), channel_id=1, source_target_pairs={{0,1},{1,2},{2,3},{4,5},{5,6},{6,7},{8,9},{9,10},{10,11},{12,13},{... | collective-permute-start | bytes 147464 | tf_op jit(solution)/shard_map/ppermute | solution.py:248
  158.3 49.2 %collective-permute-start.3 = (bf16[1,96,256]{2,1,0:T(8,128)(2,1)S(1)}, bf16[1,96,256]{2,1,0:T(8,128)(2,1)S(1)}, u32[]{:S(2)}, u32[]{:S(2)}) collective-permute-start(bf16[1,96,256]{2,1,0:T(8,128)(2,1)S(1)} %get-tuple-element.17), channel_id=1, source_target_pairs={{1,0},{2,1},{3,2},{5,4},{6,5},{7,6},{9,8},{10,9},{11,10},{13,12},{... | collective-permute-start | bytes 147464 | tf_op jit(solution)/shard_map/ppermute | solution.py:248
Sparse Core Ops, SparseCore 0:
  99.6 64.2 all-reduce.5
  166.8 40.2 all-reduce.3

commit v2 on v1

v2 whole, which is shorter than its diff:
```python
import functools
import math

import jax
import jax.numpy as jnp
from jax import lax
from jax.experimental import pallas as pl
from jax.experimental.pallas import tpu as pltpu
from jax.sharding import PartitionSpec as P

LO = 256
BF = jnp.bfloat16
F32 = jnp.float32
VMEM_LIMIT = 56 * 1024 * 1024


def split_index(index):
    return index >> 8, index & (LO - 1)


def one_hot(lo):
    rows = lax.broadcasted_iota(jnp.int32, (LO, lo.shape[1]), 0)
    return jnp.where(rows == lo, 1.0, 0.0).astype(BF)


def pick(blocks, index):
    count, channels, _ = blocks.shape
    hi, lo = split_index(index)
    found = jnp.dot(
        blocks.reshape(count * channels, LO), one_hot(lo), preferred_element_type=F32
    ).reshape(count, channels, index.shape[1])
    got = jnp.zeros((channels, index.shape[1]), F32)
    for h in range(count):
        got = jnp.where(hi == h, found[h], got)
    return got.astype(BF)


def spread(values, index, first, count):
    channels, width = values.shape
    hi, lo = split_index(index)
    parts = [values * jnp.where(hi == first + h, 1.0, 0.0).astype(BF) for h in range(count)]
    wide = jnp.concatenate(parts, axis=0)
    added = lax.dot_general(
        wide, one_hot(lo), (((1,), (1,)), ((), ())), preferred_element_type=F32
    )
    return added.reshape(count, channels, LO)


def whole(array_or_shape):
    shape = array_or_shape.shape
    return pl.BlockSpec(shape, lambda *_: (0,) * len(shape))


def params():
    return pltpu.CompilerParams(vmem_limit_bytes=VMEM_LIMIT)


def fill_blocks(blocks, own_ref, *rest):
    count = own_ref.shape[1] // LO
    for h in range(count):
        blocks[h] = own_ref[:, h * LO : (h + 1) * LO]
    at = count
    for ref in rest:
        blocks[at : at + ref.shape[0]] = ref[...]
        at += ref.shape[0]


def pick_kernel(*refs):
    index_ref, out_ref, blocks = refs[-3], refs[-2], refs[-1]
    fill_blocks(blocks, *refs[:-3])
    for b in range(out_ref.shape[0]):
        out_ref[b] = pick(blocks[...], index_ref[:, b * LO : (b + 1) * LO])


def pick_blocks(own, rest, index):
    channels, slots = own.shape
    width = index.shape[0]
    count = slots // LO + sum(r.shape[0] for r in rest)
    return pl.pallas_call(
        pick_kernel,
        out_shape=jax.ShapeDtypeStruct((width // LO, channels, LO), BF),
        scratch_shapes=[pltpu.VMEM((count, channels, LO), BF)],
        compiler_params=params(),
        name="pick_columns",
    )(own, *rest, index.reshape(1, width))


def conv_kernel(own_ref, z_ref, xy_ref, wt_ref, index_ref, up_ref, out_ref, wg_ref, blocks, got):
    k = pl.program_id(0)
    channels, slots = own_ref.shape

    @pl.when(k == 0)
    def _():
        fill_blocks(blocks, own_ref, z_ref, xy_ref)

    rows = pl.ds(pl.multiple_of(k * channels, 32), channels)
    got[rows, :] = pick(blocks[...], index_ref[0])

    @pl.when(k == pl.num_programs(0) - 1)
    def _():
        out_ref[...] = jnp.dot(wt_ref[...], got[...], preferred_element_type=F32).astype(BF)
        wg_ref[...] = lax.dot_general(
            up_ref[...], got[...], (((1,), (1,)), ((), ())), preferred_element_type=F32
        )


def convolve(own, z_blocks, xy_blocks, weight_t, index, up):
    channels, slots = own.shape
    offsets = index.shape[0]
    count = slots // LO + z_blocks.shape[0] + xy_blocks.shape[0]
    flops = 2 * offsets * slots * channels * (count * LO + 2 * channels)
    return pl.pallas_call(
        conv_kernel,
        grid=(offsets,),
        in_specs=[
            whole(own),
            whole(z_blocks),
            whole(xy_blocks),
            whole(weight_t),
            pl.BlockSpec((1, 1, slots), lambda k: (k, 0, 0)),
            whole(up),
        ],
        out_specs=[
            pl.BlockSpec((channels, slots), lambda k: (0, 0)),
            pl.BlockSpec((channels, offsets * channels), lambda k: (0, 0)),
        ],
        out_shape=[
            jax.ShapeDtypeStruct((channels, slots), BF),
            jax.ShapeDtypeStruct((channels, offsets * channels), F32),
        ],
        scratch_shapes=[
            pltpu.VMEM((count, channels, LO), BF),
            pltpu.VMEM((offsets * channels, slots), BF),
        ],
        compiler_params=params(),
        cost_estimate=pl.CostEstimate(flops=flops, bytes_accessed=4 << 20, transcendentals=0),
        name="convolve",
    )(own, z_blocks, xy_blocks, weight_t, index, up)


def spread_step(w_ref, index_ref, up_ref, back, first, count):
    k = pl.program_id(0)
    channels = up_ref.shape[0]

    @pl.when(k == 0)
    def _():
        back[...] = jnp.dot(w_ref[...], up_ref[...], preferred_element_type=F32).astype(BF)

    rows = pl.ds(pl.multiple_of(k * channels, 32), channels)
    return spread(back[rows, :], index_ref[0], first, count)


def spread_kernel(first, w_ref, index_ref, up_ref, *refs):
    acc_ref, back = refs[-2:]
    part = spread_step(w_ref, index_ref, up_ref, back, first, acc_ref.shape[0])

    @pl.when(pl.program_id(0) == 0)
    def _():
        acc_ref[...] = part + refs[0][...] if len(refs) == 3 else part

    @pl.when(pl.program_id(0) > 0)
    def _():
        acc_ref[...] += part


def spread_last_kernel(
    w_ref, index_ref, up_ref, start_ref, ext_ref, z_ref, z_index_ref, out_ref, back, acc
):
    count = acc.shape[0]

    @pl.when(pl.program_id(0) == 0)
    def _():
        acc[...] = start_ref[...] + ext_ref[...] + spread_pairs(z_ref, z_index_ref, count)

    acc[...] += spread_step(w_ref, index_ref, up_ref, back, 0, count)

    @pl.when(pl.program_id(0) == pl.num_programs(0) - 1)
    def _():
        for h in range(count):
            out_ref[:, h * LO : (h + 1) * LO] = acc[h]


def spread_specs(weight, up, begin, end):
    channels, slots = up.shape
    steps = end - begin
    return [
        pl.BlockSpec((steps * channels, channels), lambda k: (0, 0)),
        pl.BlockSpec((1, 1, slots), lambda k: (k + begin, 0, 0)),
        whole(up),
    ]


def spread_cost(up, count, steps):
    channels, slots = up.shape
    flops = 2 * steps * slots * channels * (count * LO + channels)
    return pl.CostEstimate(flops=flops, bytes_accessed=2 << 20, transcendentals=0)


def weight_rows(weight, begin, end):
    return weight[begin:end].reshape(-1, weight.shape[2])


def spread_grads(weight, index, up, first, count, begin, end, start=None):
    channels, slots = up.shape
    extra = () if start is None else (start,)
    steps = end - begin
    return pl.pallas_call(
        functools.partial(spread_kernel, first),
        grid=(steps,),
        in_specs=spread_specs(weight, up, begin, end) + [whole(e) for e in extra],
        out_specs=pl.BlockSpec((count, channels, LO), lambda k: (0, 0, 0)),
        out_shape=jax.ShapeDtypeStruct((count, channels, LO), F32),
        scratch_shapes=[pltpu.VMEM((steps * channels, slots), BF)],
        compiler_params=params(),
        cost_estimate=spread_cost(up, count, steps),
        name="spread_grads",
    )(weight_rows(weight, begin, end), index, up, *extra)


def spread_last(weight, index, up, begin, end, start, ext, z_pairs, z_index):
    count, channels, _ = start.shape
    slots = up.shape[1]
    steps = end - begin
    return pl.pallas_call(
        spread_last_kernel,
        grid=(steps,),
        in_specs=spread_specs(weight, up, begin, end)
        + [
            whole(start),
            pl.BlockSpec(start.shape, lambda k: (0, 0, 0)),
            whole(z_pairs),
            pl.BlockSpec((1, z_index.shape[0]), lambda k: (0, 0)),
        ],
        out_specs=pl.BlockSpec((channels, slots), lambda k: (0, 0)),
        out_shape=jax.ShapeDtypeStruct((channels, slots), F32),
        scratch_shapes=[
            pltpu.VMEM((steps * channels, slots), BF),
            pltpu.VMEM((count, channels, LO), F32),
        ],
        compiler_params=params(),
        cost_estimate=spread_cost(up, count, steps),
        name="spread_last",
    )(weight_rows(weight, begin, end), index, up, start, ext, z_pairs, z_index.reshape(1, -1))


def split_pair(value):
    high = value.astype(BF)
    low = (value - high.astype(F32)).astype(BF)
    return jnp.concatenate([high, low], axis=1)


def spread_pairs(pairs_ref, index_ref, count):
    channels = pairs_ref.shape[1] // 2
    index = jnp.concatenate([index_ref[...], index_ref[...]], axis=1)
    blocks = range(pairs_ref.shape[0])
    values = [pairs_ref[b, :channels, :] for b in blocks] + [
        pairs_ref[b, channels:, :] for b in blocks
    ]
    return spread(jnp.concatenate(values, axis=1), index, 0, count)


def halo_add_kernel(slots, pairs_ref, index_ref, halo_ref, ext_ref, z_ref):
    own_count = slots // LO
    z_count, channels, _ = z_ref.shape[0], ext_ref.shape[1], LO
    part = spread_pairs(pairs_ref, index_ref, own_count + z_count)
    ext_ref[...] = part[:own_count]
    z_ref[...] = split_pair(part[own_count:] + halo_ref[:z_count])


def halo_add(pairs, index, halo, own_count, z_count):
    channels = halo.shape[1]
    return pl.pallas_call(
        functools.partial(halo_add_kernel, own_count * LO),
        out_shape=[
            jax.ShapeDtypeStruct((own_count, channels, LO), F32),
            jax.ShapeDtypeStruct((z_count, 2 * channels, LO), BF),
        ],
        compiler_params=params(),
        name="halo_add",
    )(pairs, index.reshape(1, -1), halo)


def exchange(blocks, peers, per_peer):
    count, channels, _ = blocks.shape
    if per_peer != LO:
        flat = blocks.transpose(1, 0, 2).reshape(channels, peers, per_peer).transpose(1, 0, 2)
    else:
        flat = blocks
    got = lax.all_to_all(flat, "xy", split_axis=0, concat_axis=0, tiled=True)
    if per_peer != LO:
        got = got.transpose(1, 0, 2).reshape(channels, count, LO).transpose(1, 0, 2)
    return got


def shift_z(low_bound, high_bound):
    count = lax.axis_size("gz")
    up = [(i, i + 1) for i in range(count - 1)]
    down = [(b, a) for a, b in up]
    return lax.ppermute(high_bound, "gz", up), lax.ppermute(low_bound, "gz", down)


def on_device(features, weight, z_send, xy_send, kernel_map, cotangent):
    channels, slots = features.shape
    offsets = weight.shape[0]
    peers = lax.axis_size("xy")
    z_list, xy_list = z_send.reshape(-1), xy_send.reshape(-1)
    z_count = z_list.shape[0] // LO
    rim = z_count // 2
    xy_count = xy_list.shape[0] // LO
    per_peer = xy_list.shape[0] // peers
    own_count = slots // LO
    ext_count = own_count + z_count
    index = kernel_map.reshape(offsets, 1, slots)

    outgoing = pick_blocks(features, (), z_list)
    below, above = shift_z(outgoing[:rim], outgoing[rim:])
    z_blocks = jnp.concatenate([below, above], axis=0)

    cotangent, outgoing = lax.optimization_barrier((cotangent, outgoing))
    halo_grad = spread_grads(
        weight, index, cotangent, own_count, z_count + xy_count, 0, offsets
    )
    z_blocks, halo_grad = lax.optimization_barrier((z_blocks, halo_grad))

    sends = pick_blocks(features, (z_blocks,), xy_list)
    both = jnp.concatenate([sends, split_pair(halo_grad[z_count:])], axis=1)
    got = exchange(both, peers, per_peer)
    own_grad = spread_grads(weight, index, cotangent, 0, own_count, 0, offsets // 3)

    xy_blocks, xy_pairs = got[:, :channels], got[:, channels:]
    ext_grad, z_pairs = halo_add(xy_pairs, xy_list, halo_grad, own_count, z_count)
    back_low, back_high = shift_z(z_pairs[:rim], z_pairs[rim:])
    z_back = jnp.concatenate([back_low, back_high], axis=0)

    weight_t = weight.transpose(2, 0, 1).reshape(channels, offsets * channels)
    xy_blocks, own_grad = lax.optimization_barrier((xy_blocks, own_grad))
    out_features, w_term = convolve(features, z_blocks, xy_blocks, weight_t, index, cotangent)

    layers = lax.axis_size("gz")
    w_scale = 1.0 / math.sqrt(slots * peers * layers)
    cotangent, w_term = lax.optimization_barrier((cotangent, w_term))
    middle = 2 * offsets // 3
    own_grad = spread_grads(
        weight, index, cotangent, 0, own_count, offsets // 3, middle, start=own_grad
    )
    if channels % (peers * layers) == 0:
        rows = channels // (peers * layers)
        terms = lax.all_to_all(
            w_term.reshape(peers * layers, rows, -1), ("xy", "gz"), 0, 0, tiled=True
        )
        own_grad, terms = lax.optimization_barrier((own_grad, terms))
        mine = jnp.sum(terms, axis=0) * w_scale
        grad_weight = lax.all_gather(mine, "gz", axis=0, tiled=True)
    else:
        part = lax.psum_scatter(w_term, "xy", scatter_dimension=0, tiled=True)
        grad_weight = lax.psum(part, "gz") * w_scale
    grad_features = spread_last(
        weight, index, cotangent, middle, offsets, own_grad, ext_grad, z_back, z_list
    )
    return (out_features, grad_features, grad_weight)


def solution(mesh):
    slab = P(None, ("parts", "xy", "gz"))
    lists = P(("parts", "xy"), "gz", None)
    return jax.shard_map(
        on_device,
        mesh=mesh,
        in_specs=(slab, P(), lists, lists, slab, slab),
        out_specs=(slab, slab, P(("parts", "xy"), None)),
        check_vma=False,
    )
```

time: 224 us -> 181 us (0.81); the launches traced: 220 us -> 181 us
  Pallas kernels: 154 us -> 130 us
  between operations: 14.7 us -> 0.7 us
  waiting for transfers between devices: 16.8 us -> 7.29 us
  blocking collectives: 0 us -> 6.94 us
    pallas_call x5 -> x6, Pallas kernels: 150 us -> 125 us  [the longest x3 55.5 us: spread_grads(): pl.pallas_call(functools.partial(spread_kernel, first), grid=(steps,), in...]
    all_to_all x2 -> x1, waiting for transfers between devices: 10.2 us -> 0.01 us  [exchange(): got = lax.all_to_all(flat, 'xy', split_axis=0, concat_axis=0, tiled=True)]
    all_to_all x0 -> x1, waiting for transfers between devices: none -> 7.28 us  [on_device(): lax.all_to_all(w_term.reshape(peers * layers, rows, -1), ('xy', 'gz'), 0,...]
    all_gather x0 -> x1, blocking collectives: none -> 6.94 us  [on_device(): grad_weight = lax.all_gather(mine, 'gz', axis=0, tiled=True)]
    all_to_all x0 -> x1, starting transfers between devices: none -> 6.87 us  [on_device(): lax.all_to_all(w_term.reshape(peers * layers, rows, -1), ('xy', 'gz'), 0,...]
    all_to_all x2 -> x1, starting transfers between devices: 10.6 us -> 4.65 us  [exchange(): got = lax.all_to_all(flat, 'xy', split_axis=0, concat_axis=0, tiled=True)]
    unnamed x16 -> x5, local copies, waits for them, and re-layouts: 6.5 us -> 0.74 us
    ppermute x2, waiting for transfers between devices: 3.46 us -> 0.01 us  [shift_z(): lax.ppermute(low_bound, 'gz', down)]
  transfers between devices with their start and end apart: 8 -> 6, of which waited for: 4 -> 1; matrix products, arithmetic and copies ran while one was open for 4% -> 3% of each run, Pallas kernels for 37% -> 33%
where the time goes in v2:
time: 181 us
  Pallas kernels  130 us (72%)
  starting transfers between devices  22.4 us (12%)
  local copies, waits for them, and re-layouts  10.2 us (6%)
  waiting for transfers between devices  7.29 us (4%)
  blocking collectives  6.94 us (4%)
  other arithmetic  3.27 us (2%)
    pallas_call x3, Pallas kernels, spread_grads(): pl.pallas_call(functools.partial(spread_kernel, first), grid=(steps,), in...  55.5 us
    pallas_call x1, Pallas kernels, convolve(): pl.pallas_call(conv_kernel, grid=(offsets,), in_specs=[whole(own), whole(...  52.4 us
    pallas_call x1, Pallas kernels, spread_last(): pl.pallas_call(spread_last_kernel, grid=(steps,), in_specs=spread_specs(w...  14.1 us
    all_to_all x1, waiting for transfers between devices, on_device(): lax.all_to_all(w_term.reshape(peers * layers, rows, -1), ('xy', 'gz'), 0,...  7.28 us
    ppermute x2, starting transfers between devices, shift_z(): lax.ppermute(high_bound, 'gz', up)  7.01 us
    all_gather x1, blocking collectives, on_device(): grad_weight = lax.all_gather(mine, 'gz', axis=0, tiled=True)  6.94 us
    all_to_all x1, starting transfers between devices, on_device(): lax.all_to_all(w_term.reshape(peers * layers, rows, -1), ('xy', 'gz'), 0,...  6.87 us
    all_to_all x1, starting transfers between devices, exchange(): got = lax.all_to_all(flat, 'xy', split_axis=0, concat_axis=0, tiled=True)  4.65 us
  transfers between devices with their start and end apart: 6, of which 1 were waited for; matrix products, arithmetic and copies ran while one was open for 3% of the time, Pallas kernels for 33%

profile of v2, /device:TPU:17, one launch (start us, length us, event | category | flops | bytes accessed | tf_op | source)
XLA Modules:
  0.0 180.5 jit_solution(8965561186876379273)
XLA Ops:
  0.6 2.0 %pick_columns.2 = bf16[2,96,256]{2,1,0:T(8,128)(2,1)} custom-call(bf16[96,2048]{1,0:T(8,128)(2,1)} %own_ref.1, s32[1,512]{1,0:T(1,128)} %bitcast.18), custom_call_target="tpu_custom_call" | custom-call | tf_op jit(solution)/shard_map/pick_columns/pallas_call | solution.py:79
  2.6 0.8 fusion.2
  3.5 3.7 %collective-permute-start = (bf16[1,96,256]{2,1,0:T(8,128)(2,1)S(1)}, bf16[1,96,256]{2,1,0:T(8,128)(2,1)S(1)}, u32[]{:S(2)}, u32[]{:S(2)}) collective-permute-start(bf16[1,96,256]{2,1,0:T(8,128)(2,1)S(1)} %get-tuple-element.36), channel_id=1, source_target_pairs={{0,1},{1,2},{2,3},{4,5},{5,6},{6,7},{8,9},{9,10},{10,11},{12,13},{... | collective-permute-start | bytes 147464 | tf_op jit(solution)/shard_map/ppermute | solution.py:299
  7.2 1.9 %collective-permute-start.1 = (bf16[1,96,256]{2,1,0:T(8,128)(2,1)S(1)}, bf16[1,96,256]{2,1,0:T(8,128)(2,1)S(1)}, u32[]{:S(2)}, u32[]{:S(2)}) collective-permute-start(bf16[1,96,256]{2,1,0:T(8,128)(2,1)S(1)} %get-tuple-element.37), channel_id=1, source_target_pairs={{1,0},{2,1},{3,2},{5,4},{6,5},{7,6},{9,8},{10,9},{11,10},{13,12},{... | collective-permute-start | bytes 147464 | tf_op jit(solution)/shard_map/ppermute | solution.py:299
  9.1 1.8 reshape.28.index_ref
  10.9 0.0 copy-start
  10.9 29.1 %spread_grads.3.halo_ref = f32[6,96,256]{2,1,0:T(8,128)} custom-call(bf16[2592,96]{1,0:T(8,128)(2,1)} %bitcast.11, s32[27,1,2048]{2,1,0:T(1,128)} %reshape.28.index_ref, bf16[96,2048]{1,0:T(8,128)(2,1)} %up_ref.4), custom_call_target="tpu_custom_call" | custom-call | flops 17326669824 | bytes 2097152 | tf_op jit(solution)/shard_map/spread_grads/pallas_call | solution.py:207
  39.9 0.0 copy-start.1
  39.9 0.0 copy-done
  39.9 1.1 copy.11.wt_ref
  41.0 0.0 collective-permute-done
  41.0 0.0 collective-permute-done.1
  41.0 0.6 pad_maximum_fusion.2.refs_1_.z_ref
  41.7 0.0 copy-done.1
  41.7 2.4 %pick_columns.3 = bf16[4,96,256]{2,1,0:T(8,128)(2,1)} custom-call(bf16[96,2048]{1,0:T(8,128)(2,1)} %own_ref.1, bf16[2,96,256]{2,1,0:T(8,128)(2,1)} %pad_maximum_fusion.2.refs_1_.z_ref, s32[1,1024]{1,0:T(1,128)} %bitcast.16), custom_call_target="tpu_custom_call" | custom-call | tf_op jit(solution)/shard_map/pick_columns/pallas_call | solution.py:79
  44.1 1.8 pad_maximum_fusion
  45.9 4.6 %all-to-all-start = ((bf16[4,288,256]{2,1,0:T(8,128)(2,1)}), bf16[4,288,256]{2,1,0:T(8,128)(2,1)S(1)}, u32[]{:S(2)}, u32[]{:S(2)}) async-start(bf16[4,288,256]{2,1,0:T(8,128)(2,1)} %pad_maximum_fusion), calls=%async_computation | async-start | bytes 1179648 | tf_op jit(solution)/shard_map/all_to_all | solution.py:289
  50.6 0.8 fusion
  51.4 13.0 %spread_grads.4.refs_0_ = f32[8,96,256]{2,1,0:T(8,128)} custom-call(bf16[864,96]{1,0:T(8,128)(2,1)} %bitcast.15, s32[27,1,2048]{2,1,0:T(1,128)} %reshape.28.index_ref, bf16[96,2048]{1,0:T(8,128)(2,1)} %up_ref.4), custom_call_target="tpu_custom_call" | custom-call | flops 7587495936 | bytes 2097152 | tf_op jit(solution)/shard_map/spread_grads/pallas_call | solution.py:207
  64.4 0.0 all-to-all-done
  64.4 0.7 slice.42.xy_ref
  65.1 52.4 %convolve.1 = (bf16[96,2048]{1,0:T(8,128)(2,1)}, f32[96,2592]{1,0:T(8,128)}) custom-call(bf16[96,2048]{1,0:T(8,128)(2,1)} %own_ref.1, bf16[2,96,256]{2,1,0:T(8,128)(2,1)} %pad_maximum_fusion.2.refs_1_.z_ref, bf16[4,96,256]{2,1,0:T(8,128)(2,1)} %slice.42.xy_ref, bf16[96,2592]{1,0:T(8,128)(2,1)} %copy.11.wt_ref, s32[27,1,2048]{2,1,0:T(1,128)} %reshape.28.index_ref, ...), custom_call_target="tpu_custom_call" | custom-call | flops 40089157632 | bytes 4194304 | tf_op jit(solution)/shard_map/convolve/pallas_call | solution.py:112
  117.6 2.4 %reshape.33 = f32[16,6,2592]{2,1,0:T(8,128)} reshape(f32[96,2592]{1,0:T(8,128)} %get-tuple-element.24) | data formatting | bytes 1990656 | tf_op jit(solution)/shard_map/reshape | solution.py:349
  120.0 6.9 %all-to-all-start.1 = ((f32[16,6,2592]{2,1,0:T(8,128)}), f32[16,6,2592]{2,1,0:T(8,128)S(1)}, u32[]{:S(2)}, u32[]{:S(2)}) async-start(f32[16,6,2592]{2,1,0:T(8,128)} %reshape.33), calls=%async_computation.1 | async-start | bytes 2752512 | tf_op jit(solution)/shard_map/all_to_all | solution.py:348
  126.9 0.8 slice.43.pairs_ref
  127.6 3.3 %halo_add.1 = (f32[8,96,256]{2,1,0:T(8,128)}, bf16[2,192,256]{2,1,0:T(8,128)(2,1)}) custom-call(bf16[4,192,256]{2,1,0:T(8,128)(2,1)} %slice.43.pairs_ref, s32[1,1024]{1,0:T(1,128)} %bitcast.17, f32[6,96,256]{2,1,0:T(8,128)} %spread_grads.3.halo_ref), custom_call_target="tpu_custom_call" | custom-call | tf_op jit(solution)/shard_map/halo_add/pallas_call | solution.py:272
  130.9 1.0 fusion.1
  131.9 3.3 %collective-permute-start.2 = (bf16[1,192,256]{2,1,0:T(8,128)(2,1)S(1)}, bf16[1,192,256]{2,1,0:T(8,128)(2,1)S(1)}, u32[]{:S(2)}, u32[]{:S(2)}) collective-permute-start(bf16[1,192,256]{2,1,0:T(8,128)(2,1)S(1)} %get-tuple-element.34), channel_id=1, source_target_pairs={{0,1},{1,2},{2,3},{4,5},{5,6},{6,7},{8,9},{9,10},{10,11},{12,13},{... | collective-permute-start | bytes 294920 | tf_op jit(solution)/shard_map/ppermute | solution.py:299
  135.2 1.9 %collective-permute-start.3 = (bf16[1,192,256]{2,1,0:T(8,128)(2,1)S(1)}, bf16[1,192,256]{2,1,0:T(8,128)(2,1)S(1)}, u32[]{:S(2)}, u32[]{:S(2)}) collective-permute-start(bf16[1,192,256]{2,1,0:T(8,128)(2,1)S(1)} %get-tuple-element.35), channel_id=1, source_target_pairs={{1,0},{2,1},{3,2},{5,4},{6,5},{7,6},{9,8},{10,9},{11,10},{13,12},{... | collective-permute-start | bytes 294920 | tf_op jit(solution)/shard_map/ppermute | solution.py:299
  137.2 13.4 %spread_grads.5.start_ref = f32[8,96,256]{2,1,0:T(8,128)} custom-call(bf16[864,96]{1,0:T(8,128)(2,1)} %bitcast.14, s32[27,1,2048]{2,1,0:T(1,128)} %reshape.28.index_ref, bf16[96,2048]{1,0:T(8,128)(2,1)} %up_ref.4, f32[8,96,256]{2,1,0:T(8,128)} %spread_grads.4.refs_0_), custom_call_target="tpu_custom_call" | custom-call | flops 7587495936 | bytes 2097152 | tf_op jit(solution)/shard_map/spread_grads/pallas_call | solution.py:207
  150.6 0.0 collective-permute-done.2
  150.6 0.0 collective-permute-done.3
  150.6 0.7 pad_maximum_fusion.1.z_ref
  151.3 7.3 %all-to-all-done.1 = f32[16,6,2592]{2,1,0:T(8,128)S(1)} async-done(((f32[16,6,2592]{2,1,0:T(8,128)}), f32[16,6,2592]{2,1,0:T(8,128)S(1)}, u32[]{:S(2)}, u32[]{:S(2)}) %all-to-all-start.1) | async-done | bytes 995360 | tf_op jit(solution)/shard_map/all_to_all | solution.py:348
  158.6 0.1 reduce_sum.9
  158.7 6.9 %all-gather = f32[4,6,2592]{2,1,0:T(8,128)S(1)} all-gather(f32[1,6,2592]{2,1,0:T(8,128)S(1)} %multiply_bitcast_fusion), channel_id=1, replica_groups=mesh['parts'=2,'xy'=4,'gz'=4] {'gz'}, dimensions={0}, use_global_device_ids=true | all-gather | bytes 311040 | tf_op jit(solution)/shard_map/all_gather | solution.py:353
  165.6 0.7 reshape.35
  166.4 14.1 %spread_last.1 = f32[96,2048]{1,0:T(8,128)} custom-call(bf16[864,96]{1,0:T(8,128)(2,1)} %bitcast.13, s32[27,1,2048]{2,1,0:T(1,128)} %reshape.28.index_ref, bf16[96,2048]{1,0:T(8,128)(2,1)} %up_ref.4, f32[8,96,256]{2,1,0:T(8,128)} %spread_grads.5.start_ref, f32[8,96,256]{2,1,0:T(8,128)} %get-tuple-element.26.ext_ref, ...), custom_call_target="tpu_custom_call" | custom-call | flops 7587495936 | bytes 2097152 | tf_op jit(solution)/shard_map/spread_last/pallas_call | solution.py:224
  (2 shorter events, 0.0 us)
Async XLA Ops:
  3.5 37.6 %collective-permute-start = (bf16[1,96,256]{2,1,0:T(8,128)(2,1)S(1)}, bf16[1,96,256]{2,1,0:T(8,128)(2,1)S(1)}, u32[]{:S(2)}, u32[]{:S(2)}) collective-permute-start(bf16[1,96,256]{2,1,0:T(8,128)(2,1)S(1)} %get-tuple-element.36), channel_id=1, source_target_pairs={{0,1},{1,2},{2,3},{4,5},{5,6},{6,7},{8,9},{9,10},{10,11},{12,13},{... | collective-permute-start | bytes 147464 | tf_op jit(solution)/shard_map/ppermute | solution.py:299
  7.2 33.9 %collective-permute-start.1 = (bf16[1,96,256]{2,1,0:T(8,128)(2,1)S(1)}, bf16[1,96,256]{2,1,0:T(8,128)(2,1)S(1)}, u32[]{:S(2)}, u32[]{:S(2)}) collective-permute-start(bf16[1,96,256]{2,1,0:T(8,128)(2,1)S(1)} %get-tuple-element.37), channel_id=1, source_target_pairs={{1,0},{2,1},{3,2},{5,4},{6,5},{7,6},{9,8},{10,9},{11,10},{13,12},{... | collective-permute-start | bytes 147464 | tf_op jit(solution)/shard_map/ppermute | solution.py:299
  10.9 29.1 %copy-start = (bf16[27,96,96]{2,1,0:T(8,128)(2,1)S(1)}, bf16[27,96,96]{2,1,0:T(8,128)(2,1)}, u32[]{:S(2)}) copy-start(bf16[27,96,96]{2,1,0:T(8,128)(2,1)} %param.7) | copy-start | bytes 1492996
  39.9 1.7 copy-start.1
  45.9 18.5 %all-to-all-start = ((bf16[4,288,256]{2,1,0:T(8,128)(2,1)}), bf16[4,288,256]{2,1,0:T(8,128)(2,1)S(1)}, u32[]{:S(2)}, u32[]{:S(2)}) async-start(bf16[4,288,256]{2,1,0:T(8,128)(2,1)} %pad_maximum_fusion), calls=%async_computation | async-start | bytes 1179648 | tf_op jit(solution)/shard_map/all_to_all | solution.py:289
  120.0 38.6 %all-to-all-start.1 = ((f32[16,6,2592]{2,1,0:T(8,128)}), f32[16,6,2592]{2,1,0:T(8,128)S(1)}, u32[]{:S(2)}, u32[]{:S(2)}) async-start(f32[16,6,2592]{2,1,0:T(8,128)} %reshape.33), calls=%async_computation.1 | async-start | bytes 2752512 | tf_op jit(solution)/shard_map/all_to_all | solution.py:348
  131.9 18.7 %collective-permute-start.2 = (bf16[1,192,256]{2,1,0:T(8,128)(2,1)S(1)}, bf16[1,192,256]{2,1,0:T(8,128)(2,1)S(1)}, u32[]{:S(2)}, u32[]{:S(2)}) collective-permute-start(bf16[1,192,256]{2,1,0:T(8,128)(2,1)S(1)} %get-tuple-element.34), channel_id=1, source_target_pairs={{0,1},{1,2},{2,3},{4,5},{5,6},{6,7},{8,9},{9,10},{10,11},{12,13},{... | collective-permute-start | bytes 294920 | tf_op jit(solution)/shard_map/ppermute | solution.py:299
  135.2 15.3 %collective-permute-start.3 = (bf16[1,192,256]{2,1,0:T(8,128)(2,1)S(1)}, bf16[1,192,256]{2,1,0:T(8,128)(2,1)S(1)}, u32[]{:S(2)}, u32[]{:S(2)}) collective-permute-start(bf16[1,192,256]{2,1,0:T(8,128)(2,1)S(1)} %get-tuple-element.35), channel_id=1, source_target_pairs={{1,0},{2,1},{3,2},{5,4},{6,5},{7,6},{9,8},{10,9},{11,10},{13,12},{... | collective-permute-start | bytes 294920 | tf_op jit(solution)/shard_map/ppermute | solution.py:299

commit v3 on v2

--- a/solution.py
+++ b/solution.py
@@ -11,6 +11,7 @@
 LO = 256
 BF = jnp.bfloat16
 F32 = jnp.float32
+GROUP = 3
 VMEM_LIMIT = 56 * 1024 * 1024
 
 
@@ -19,8 +20,8 @@
 
 
 def one_hot(lo):
-    rows = lax.broadcasted_iota(jnp.int32, (LO, lo.shape[1]), 0)
-    return jnp.where(rows == lo, 1.0, 0.0).astype(BF)
+    rows = lax.broadcasted_iota(jnp.int32, (LO, lo.shape[1]), 0).astype(BF)
+    return jnp.where(rows == lo.astype(BF), jnp.array(1, BF), jnp.array(0, BF))
 
 
 def pick(blocks, index):
@@ -93,40 +94,45 @@
     def _():
         fill_blocks(blocks, own_ref, z_ref, xy_ref)
 
-    rows = pl.ds(pl.multiple_of(k * channels, 32), channels)
-    got[rows, :] = pick(blocks[...], index_ref[0])
+    for i in range(GROUP):
+        at = k * GROUP + i
+        rows = pl.ds(pl.multiple_of(at * channels, 32), channels)
+        got[rows, :] = pick(blocks[...], index_ref[pl.ds(at, 1), :])
 
     @pl.when(k == pl.num_programs(0) - 1)
     def _():
         out_ref[...] = jnp.dot(wt_ref[...], got[...], preferred_element_type=F32).astype(BF)
-        wg_ref[...] = lax.dot_general(
+        term = lax.dot_general(
             up_ref[...], got[...], (((1,), (1,)), ((), ())), preferred_element_type=F32
         )
-
-
-def convolve(own, z_blocks, xy_blocks, weight_t, index, up):
+        height = wg_ref.shape[1]
+        for p in range(wg_ref.shape[0]):
+            wg_ref[p] = term[p * height : (p + 1) * height]
+
+
+def convolve(own, z_blocks, xy_blocks, weight_t, index, up, pieces):
     channels, slots = own.shape
     offsets = index.shape[0]
     count = slots // LO + z_blocks.shape[0] + xy_blocks.shape[0]
     flops = 2 * offsets * slots * channels * (count * LO + 2 * channels)
     return pl.pallas_call(
         conv_kernel,
-        grid=(offsets,),
+        grid=(offsets // GROUP,),
         in_specs=[
             whole(own),
             whole(z_blocks),
             whole(xy_blocks),
             whole(weight_t),
-            pl.BlockSpec((1, 1, slots), lambda k: (k, 0, 0)),
+            whole(index),
             whole(up),
         ],
         out_specs=[
             pl.BlockSpec((channels, slots), lambda k: (0, 0)),
-            pl.BlockSpec((channels, offsets * channels), lambda k: (0, 0)),
+            pl.BlockSpec((pieces, channels // pieces, offsets * channels), lambda k: (0, 0, 0)),
         ],
         out_shape=[
             jax.ShapeDtypeStruct((channels, slots), BF),
-            jax.ShapeDtypeStruct((channels, offsets * channels), F32),
+            jax.ShapeDtypeStruct((pieces, channels // pieces, offsets * channels), F32),
         ],
         scratch_shapes=[
             pltpu.VMEM((count, channels, LO), BF),
@@ -138,7 +144,7 @@
     )(own, z_blocks, xy_blocks, weight_t, index, up)
 
 
-def spread_step(w_ref, index_ref, up_ref, back, first, count):
+def spread_step(w_ref, index_ref, up_ref, back, first, count, begin):
     k = pl.program_id(0)
     channels = up_ref.shape[0]
 
@@ -146,13 +152,18 @@
     def _():
         back[...] = jnp.dot(w_ref[...], up_ref[...], preferred_element_type=F32).astype(BF)
 
-    rows = pl.ds(pl.multiple_of(k * channels, 32), channels)
-    return spread(back[rows, :], index_ref[0], first, count)
-
-
-def spread_kernel(first, w_ref, index_ref, up_ref, *refs):
+    total = None
+    for i in range(GROUP):
+        at = k * GROUP + i
+        rows = pl.ds(pl.multiple_of(at * channels, 32), channels)
+        part = spread(back[rows, :], index_ref[pl.ds(begin + at, 1), :], first, count)
+        total = part if total is None else total + part
+    return total
+
+
+def spread_kernel(first, begin, w_ref, index_ref, up_ref, *refs):
     acc_ref, back = refs[-2:]
-    part = spread_step(w_ref, index_ref, up_ref, back, first, acc_ref.shape[0])
+    part = spread_step(w_ref, index_ref, up_ref, back, first, acc_ref.shape[0], begin)
 
     @pl.when(pl.program_id(0) == 0)
     def _():
@@ -164,7 +175,7 @@
 
 
 def spread_last_kernel(
-    w_ref, index_ref, up_ref, start_ref, ext_ref, z_ref, z_index_ref, out_ref, back, acc
+    begin, w_ref, index_ref, up_ref, start_ref, ext_ref, z_ref, z_index_ref, out_ref, back, acc
 ):
     count = acc.shape[0]
 
@@ -172,7 +183,7 @@
     def _():
         acc[...] = start_ref[...] + ext_ref[...] + spread_pairs(z_ref, z_index_ref, count)
 
-    acc[...] += spread_step(w_ref, index_ref, up_ref, back, 0, count)
+    acc[...] += spread_step(w_ref, index_ref, up_ref, back, 0, count, begin)
 
     @pl.when(pl.program_id(0) == pl.num_programs(0) - 1)
     def _():
@@ -180,12 +191,12 @@
             out_ref[:, h * LO : (h + 1) * LO] = acc[h]
 
 
-def spread_specs(weight, up, begin, end):
+def spread_specs(weight, index, up, begin, end):
     channels, slots = up.shape
     steps = end - begin
     return [
         pl.BlockSpec((steps * channels, channels), lambda k: (0, 0)),
-        pl.BlockSpec((1, 1, slots), lambda k: (k + begin, 0, 0)),
+        whole(index),
         whole(up),
     ]
 
@@ -205,9 +216,9 @@
     extra = () if start is None else (start,)
     steps = end - begin
     return pl.pallas_call(
-        functools.partial(spread_kernel, first),
-        grid=(steps,),
-        in_specs=spread_specs(weight, up, begin, end) + [whole(e) for e in extra],
+        functools.partial(spread_kernel, first, begin),
+        grid=(steps // GROUP,),
+        in_specs=spread_specs(weight, index, up, begin, end) + [whole(e) for e in extra],
         out_specs=pl.BlockSpec((count, channels, LO), lambda k: (0, 0, 0)),
         out_shape=jax.ShapeDtypeStruct((count, channels, LO), F32),
         scratch_shapes=[pltpu.VMEM((steps * channels, slots), BF)],
@@ -222,9 +233,9 @@
     slots = up.shape[1]
     steps = end - begin
     return pl.pallas_call(
-        spread_last_kernel,
-        grid=(steps,),
-        in_specs=spread_specs(weight, up, begin, end)
+        functools.partial(spread_last_kernel, begin),
+        grid=(steps // GROUP,),
+        in_specs=spread_specs(weight, index, up, begin, end)
         + [
             whole(start),
             pl.BlockSpec(start.shape, lambda k: (0, 0, 0)),
@@ -310,7 +321,7 @@
     per_peer = xy_list.shape[0] // peers
     own_count = slots // LO
     ext_count = own_count + z_count
-    index = kernel_map.reshape(offsets, 1, slots)
+    index = kernel_map
 
     outgoing = pick_blocks(features, (), z_list)
     below, above = shift_z(outgoing[:rim], outgoing[rim:])
@@ -334,25 +345,33 @@
 
     weight_t = weight.transpose(2, 0, 1).reshape(channels, offsets * channels)
     xy_blocks, own_grad = lax.optimization_barrier((xy_blocks, own_grad))
-    out_features, w_term = convolve(features, z_blocks, xy_blocks, weight_t, index, cotangent)
-
     layers = lax.axis_size("gz")
+    even = channels % (peers * layers) == 0
+    out_features, w_term = convolve(
+        features,
+        z_blocks,
+        xy_blocks,
+        weight_t,
+        index,
+        cotangent,
+        peers * layers if even else 1,
+    )
+
     w_scale = 1.0 / math.sqrt(slots * peers * layers)
     cotangent, w_term = lax.optimization_barrier((cotangent, w_term))
     middle = 2 * offsets // 3
     own_grad = spread_grads(
         weight, index, cotangent, 0, own_count, offsets // 3, middle, start=own_grad
     )
-    if channels % (peers * layers) == 0:
-        rows = channels // (peers * layers)
-        terms = lax.all_to_all(
-            w_term.reshape(peers * layers, rows, -1), ("xy", "gz"), 0, 0, tiled=True
-        )
+    if even:
+        terms = lax.all_to_all(w_term, ("xy", "gz"), 0, 0, tiled=True)
         own_grad, terms = lax.optimization_barrier((own_grad, terms))
         mine = jnp.sum(terms, axis=0) * w_scale
-        grad_weight = lax.all_gather(mine, "gz", axis=0, tiled=True)
+        spread_out = jnp.broadcast_to(mine, (layers,) + mine.shape)
+        rows = lax.all_to_all(spread_out, "gz", 0, 0, tiled=True)
+        grad_weight = rows.reshape(-1, rows.shape[2])
     else:
-        part = lax.psum_scatter(w_term, "xy", scatter_dimension=0, tiled=True)
+        part = lax.psum_scatter(w_term[0], "xy", scatter_dimension=0, tiled=True)
         grad_weight = lax.psum(part, "gz") * w_scale
     grad_features = spread_last(
         weight, index, cotangent, middle, offsets, own_grad, ext_grad, z_back, z_list

time: 181 us -> 164 us (0.906)
  Pallas kernels: 130 us -> 117 us
  blocking collectives: 6.94 us -> 0 us
  starting transfers between devices: 22.4 us -> 27.1 us
  local copies, waits for them, and re-layouts: 10.2 us -> 6.68 us
    pallas_call x5, Pallas kernels: 122 us -> 109 us  [the longest x1 49.3 us: convolve(): pl.pallas_call(conv_kernel, grid=(offsets // GROUP,), in_specs=[whole(own...]
    all_gather x1 -> x0, blocking collectives: 6.94 us -> none  [on_device(): grad_weight = lax.all_gather(mine, 'gz', axis=0, tiled=True)]
    all_to_all x1 -> x2, starting transfers between devices: 6.87 us -> 11.4 us  [the longest x1 7.06 us: on_device(): terms = lax.all_to_all(w_term, ('xy', 'gz'), 0, 0, tiled=True)]
    reshape x2 -> x1, local copies, waits for them, and re-layouts: 4.24 us -> 0.74 us  [on_device(): grad_weight = rows.reshape(-1, rows.shape[2])]
    all_to_all x1 -> x2, waiting for transfers between devices: 7.28 us -> 8.77 us  [the longest x1 8.77 us: on_device(): terms = lax.all_to_all(w_term, ('xy', 'gz'), 0, 0, tiled=True)]
  transfers between devices with their start and end apart: 6 -> 7, of which waited for: 1 -> 2; matrix products, arithmetic and copies ran while one was open for 3% -> 3% of each run, Pallas kernels for 33% -> 39%
where the time goes in v3:
time: 164 us; the launch traced here: 163 us
  Pallas kernels  117 us (71%)
  starting transfers between devices  27.1 us (17%)
  waiting for transfers between devices  8.92 us (5%)
  local copies, waits for them, and re-layouts  6.68 us (4%)
  other arithmetic  3.27 us (2%)
    pallas_call x1, Pallas kernels, convolve(): pl.pallas_call(conv_kernel, grid=(offsets // GROUP,), in_specs=[whole(own...  49.3 us
    pallas_call x3, Pallas kernels, spread_grads(): pl.pallas_call(functools.partial(spread_kernel, first, begin), grid=(step...  47 us
    pallas_call x1, Pallas kernels, spread_last(): pl.pallas_call(functools.partial(spread_last_kernel, begin), grid=(steps...  12.5 us
    all_to_all x1, waiting for transfers between devices, on_device(): terms = lax.all_to_all(w_term, ('xy', 'gz'), 0, 0, tiled=True)  8.77 us
    all_to_all x1, starting transfers between devices, on_device(): terms = lax.all_to_all(w_term, ('xy', 'gz'), 0, 0, tiled=True)  7.06 us
    ppermute x2, starting transfers between devices, shift_z(): lax.ppermute(high_bound, 'gz', up)  7.01 us
    all_to_all x1, starting transfers between devices, exchange(): got = lax.all_to_all(flat, 'xy', split_axis=0, concat_axis=0, tiled=True)  4.65 us
    pallas_call x2, Pallas kernels, pick_blocks(): pl.pallas_call(pick_kernel, out_shape=jax.ShapeDtypeStruct((width // LO,...  4.43 us
  transfers between devices with their start and end apart: 7, of which 2 were waited for; matrix products, arithmetic and copies ran while one was open for 3% of the time, Pallas kernels for 39%

profile of v3, /device:TPU:17, one launch (start us, length us, event | category | flops | bytes accessed | tf_op | source)
XLA Modules:
  0.0 163.2 jit_solution(12947288949463387899)
XLA Ops:
  0.6 2.0 %pick_columns.2 = bf16[2,96,256]{2,1,0:T(8,128)(2,1)} custom-call(bf16[96,2048]{1,0:T(8,128)(2,1)} %own_ref.1, s32[1,512]{1,0:T(1,128)} %bitcast.16), custom_call_target="tpu_custom_call" | custom-call | tf_op jit(solution)/shard_map/pick_columns/pallas_call | solution.py:80
  2.6 0.8 fusion.2
  3.5 3.7 %collective-permute-start = (bf16[1,96,256]{2,1,0:T(8,128)(2,1)S(1)}, bf16[1,96,256]{2,1,0:T(8,128)(2,1)S(1)}, u32[]{:S(2)}, u32[]{:S(2)}) collective-permute-start(bf16[1,96,256]{2,1,0:T(8,128)(2,1)S(1)} %get-tuple-element.36), channel_id=1, source_target_pairs={{0,1},{1,2},{2,3},{4,5},{5,6},{6,7},{8,9},{9,10},{10,11},{12,13},{... | collective-permute-start | bytes 147464 | tf_op jit(solution)/shard_map/ppermute | solution.py:310
  7.2 1.9 %collective-permute-start.1 = (bf16[1,96,256]{2,1,0:T(8,128)(2,1)S(1)}, bf16[1,96,256]{2,1,0:T(8,128)(2,1)S(1)}, u32[]{:S(2)}, u32[]{:S(2)}) collective-permute-start(bf16[1,96,256]{2,1,0:T(8,128)(2,1)S(1)} %get-tuple-element.37), channel_id=1, source_target_pairs={{1,0},{2,1},{3,2},{5,4},{6,5},{7,6},{9,8},{10,9},{11,10},{13,12},{... | collective-permute-start | bytes 147464 | tf_op jit(solution)/shard_map/ppermute | solution.py:310
  9.1 0.0 copy-start
  9.1 24.1 %spread_grads.3.halo_ref = f32[6,96,256]{2,1,0:T(8,128)} custom-call(bf16[2592,96]{1,0:T(8,128)(2,1)} %bitcast.9, s32[27,2048]{1,0:T(8,128)} %index_ref.9, bf16[96,2048]{1,0:T(8,128)(2,1)} %up_ref.4), custom_call_target="tpu_custom_call" | custom-call | flops 17326669824 | bytes 2097152 | tf_op jit(solution)/shard_map/spread_grads/pallas_call | solution.py:218
  33.2 0.0 copy-start.1
  33.2 0.0 copy-done
  33.2 1.1 copy.10.wt_ref
  34.3 0.0 collective-permute-done
  34.3 0.0 collective-permute-done.1
  34.3 0.6 pad_maximum_fusion.2.refs_1_.z_ref
  34.9 0.0 copy-done.1
  35.0 2.4 %pick_columns.3 = bf16[4,96,256]{2,1,0:T(8,128)(2,1)} custom-call(bf16[96,2048]{1,0:T(8,128)(2,1)} %own_ref.1, bf16[2,96,256]{2,1,0:T(8,128)(2,1)} %pad_maximum_fusion.2.refs_1_.z_ref, s32[1,1024]{1,0:T(1,128)} %bitcast.14), custom_call_target="tpu_custom_call" | custom-call | tf_op jit(solution)/shard_map/pick_columns/pallas_call | solution.py:80
  37.4 1.8 %pad_maximum_fusion = bf16[4,288,256]{2,1,0:T(8,128)(2,1)} fusion(bf16[4,96,256]{2,1,0:T(8,128)(2,1)S(1)} %get-tuple-element.29, bf16[4,96,256]{2,1,0:T(8,128)(2,1)S(1)} %get-tuple-element.30, bf16[4,96,256]{2,1,0:T(8,128)(2,1)} %pick_columns.3), kind=kLoop, calls=%fused_computation | loop fusion | flops 1769472 | bytes 1179648 | tf_op jit(solution)/shard_map/concatenate | solution.py:337
  39.2 4.7 %all-to-all-start = ((bf16[4,288,256]{2,1,0:T(8,128)(2,1)}), bf16[4,288,256]{2,1,0:T(8,128)(2,1)S(1)}, u32[]{:S(2)}, u32[]{:S(2)}) async-start(bf16[4,288,256]{2,1,0:T(8,128)(2,1)} %pad_maximum_fusion), calls=%async_computation | async-start | bytes 1179648 | tf_op jit(solution)/shard_map/all_to_all | solution.py:300
  43.8 0.9 fusion
  44.7 11.3 %spread_grads.4.refs_0_ = f32[8,96,256]{2,1,0:T(8,128)} custom-call(bf16[864,96]{1,0:T(8,128)(2,1)} %bitcast.13, s32[27,2048]{1,0:T(8,128)} %index_ref.9, bf16[96,2048]{1,0:T(8,128)(2,1)} %up_ref.4), custom_call_target="tpu_custom_call" | custom-call | flops 7587495936 | bytes 2097152 | tf_op jit(solution)/shard_map/spread_grads/pallas_call | solution.py:218
  56.0 0.1 all-to-all-done
  56.1 0.7 slice.42.xy_ref
  56.8 49.3 %convolve.1 = (bf16[96,2048]{1,0:T(8,128)(2,1)}, f32[16,6,2592]{2,1,0:T(8,128)}) custom-call(bf16[96,2048]{1,0:T(8,128)(2,1)} %own_ref.1, bf16[2,96,256]{2,1,0:T(8,128)(2,1)} %pad_maximum_fusion.2.refs_1_.z_ref, bf16[4,96,256]{2,1,0:T(8,128)(2,1)} %slice.42.xy_ref, bf16[96,2592]{1,0:T(8,128)(2,1)} %copy.10.wt_ref, s32[27,2048]{1,0:T(8,128)} %index_ref.9, ...), custom_call_target="tpu_custom_call" | custom-call | flops 40089157632 | bytes 4194304 | tf_op jit(solution)/shard_map/convolve/pallas_call | solution.py:118
  106.1 7.1 %all-to-all-start.1 = ((f32[16,6,2592]{2,1,0:T(8,128)}), f32[16,6,2592]{2,1,0:T(8,128)S(1)}, u32[]{:S(2)}, u32[]{:S(2)}) async-start(f32[16,6,2592]{2,1,0:T(8,128)} %get-tuple-element.24), calls=%async_computation.1 | async-start | bytes 2752512 | tf_op jit(solution)/shard_map/all_to_all | solution.py:367
  113.1 0.8 slice.43.pairs_ref
  113.9 3.3 %halo_add.1 = (f32[8,96,256]{2,1,0:T(8,128)}, bf16[2,192,256]{2,1,0:T(8,128)(2,1)}) custom-call(bf16[4,192,256]{2,1,0:T(8,128)(2,1)} %slice.43.pairs_ref, s32[1,1024]{1,0:T(1,128)} %bitcast.15, f32[6,96,256]{2,1,0:T(8,128)} %spread_grads.3.halo_ref), custom_call_target="tpu_custom_call" | custom-call | tf_op jit(solution)/shard_map/halo_add/pallas_call | solution.py:283
  117.3 1.0 fusion.1
  118.2 3.3 %collective-permute-start.2 = (bf16[1,192,256]{2,1,0:T(8,128)(2,1)S(1)}, bf16[1,192,256]{2,1,0:T(8,128)(2,1)S(1)}, u32[]{:S(2)}, u32[]{:S(2)}) collective-permute-start(bf16[1,192,256]{2,1,0:T(8,128)(2,1)S(1)} %get-tuple-element.34), channel_id=1, source_target_pairs={{0,1},{1,2},{2,3},{4,5},{5,6},{6,7},{8,9},{9,10},{10,11},{12,13},{... | collective-permute-start | bytes 294920 | tf_op jit(solution)/shard_map/ppermute | solution.py:310
  121.6 2.1 %collective-permute-start.3 = (bf16[1,192,256]{2,1,0:T(8,128)(2,1)S(1)}, bf16[1,192,256]{2,1,0:T(8,128)(2,1)S(1)}, u32[]{:S(2)}, u32[]{:S(2)}) collective-permute-start(bf16[1,192,256]{2,1,0:T(8,128)(2,1)S(1)} %get-tuple-element.35), channel_id=1, source_target_pairs={{1,0},{2,1},{3,2},{5,4},{6,5},{7,6},{9,8},{10,9},{11,10},{13,12},{... | collective-permute-start | bytes 294920 | tf_op jit(solution)/shard_map/ppermute | solution.py:310
  123.7 11.6 %spread_grads.5.start_ref = f32[8,96,256]{2,1,0:T(8,128)} custom-call(bf16[864,96]{1,0:T(8,128)(2,1)} %bitcast.12, s32[27,2048]{1,0:T(8,128)} %index_ref.9, bf16[96,2048]{1,0:T(8,128)(2,1)} %up_ref.4, f32[8,96,256]{2,1,0:T(8,128)} %spread_grads.4.refs_0_), custom_call_target="tpu_custom_call" | custom-call | flops 7587495936 | bytes 2097152 | tf_op jit(solution)/shard_map/spread_grads/pallas_call | solution.py:218
  135.3 0.0 collective-permute-done.2
  135.3 0.0 collective-permute-done.3
  135.3 0.7 pad_maximum_fusion.1.z_ref
  136.0 8.8 %all-to-all-done.1 = f32[16,6,2592]{2,1,0:T(8,128)S(1)} async-done(((f32[16,6,2592]{2,1,0:T(8,128)}), f32[16,6,2592]{2,1,0:T(8,128)S(1)}, u32[]{:S(2)}, u32[]{:S(2)}) %all-to-all-start.1) | async-done | bytes 995360 | tf_op jit(solution)/shard_map/all_to_all | solution.py:367
  144.8 0.1 reduce_sum.9
  144.9 0.7 broadcast_in_dim.3
  145.7 4.3 %all-to-all-start.2 = ((f32[4,6,2592]{2,1,0:T(8,128)}), f32[4,6,2592]{2,1,0:T(8,128)S(1)}, u32[]{:S(2)}, u32[]{:S(2)}) async-start(f32[4,6,2592]{2,1,0:T(8,128)} %broadcast_in_dim.3), calls=%async_computation.2 | async-start | bytes 688128 | tf_op jit(solution)/shard_map/all_to_all | solution.py:371
  150.0 12.5 %spread_last.1 = f32[96,2048]{1,0:T(8,128)} custom-call(bf16[864,96]{1,0:T(8,128)(2,1)} %bitcast.11, s32[27,2048]{1,0:T(8,128)} %index_ref.9, bf16[96,2048]{1,0:T(8,128)(2,1)} %up_ref.4, f32[8,96,256]{2,1,0:T(8,128)} %spread_grads.5.start_ref, f32[8,96,256]{2,1,0:T(8,128)} %get-tuple-element.26.ext_ref, bf16[2,192,256]{2,1,0:T(8,128)(2,1)} %pad_maximum_fusion.1.z_ref, ...), custom_call_target="tpu_custom_call" | custom-call | flops 7587495936 | bytes 2097152 | tf_op jit(solution)/shard_map/spread_last/pallas_call | solution.py:235
  162.4 0.0 all-to-all-done.2
  162.5 0.7 reshape.29
  (2 shorter events, 0.0 us)
Async XLA Ops:
  3.5 30.8 %collective-permute-start = (bf16[1,96,256]{2,1,0:T(8,128)(2,1)S(1)}, bf16[1,96,256]{2,1,0:T(8,128)(2,1)S(1)}, u32[]{:S(2)}, u32[]{:S(2)}) collective-permute-start(bf16[1,96,256]{2,1,0:T(8,128)(2,1)S(1)} %get-tuple-element.36), channel_id=1, source_target_pairs={{0,1},{1,2},{2,3},{4,5},{5,6},{6,7},{8,9},{9,10},{10,11},{12,13},{... | collective-permute-start | bytes 147464 | tf_op jit(solution)/shard_map/ppermute | solution.py:310
  7.2 27.1 %collective-permute-start.1 = (bf16[1,96,256]{2,1,0:T(8,128)(2,1)S(1)}, bf16[1,96,256]{2,1,0:T(8,128)(2,1)S(1)}, u32[]{:S(2)}, u32[]{:S(2)}) collective-permute-start(bf16[1,96,256]{2,1,0:T(8,128)(2,1)S(1)} %get-tuple-element.37), channel_id=1, source_target_pairs={{1,0},{2,1},{3,2},{5,4},{6,5},{7,6},{9,8},{10,9},{11,10},{13,12},{... | collective-permute-start | bytes 147464 | tf_op jit(solution)/shard_map/ppermute | solution.py:310
  9.1 24.1 %copy-start = (bf16[27,96,96]{2,1,0:T(8,128)(2,1)S(1)}, bf16[27,96,96]{2,1,0:T(8,128)(2,1)}, u32[]{:S(2)}) copy-start(bf16[27,96,96]{2,1,0:T(8,128)(2,1)} %param.7) | copy-start | bytes 1492996
  33.2 1.7 %copy-start.1 = (f32[6,96,256]{2,1,0:T(8,128)S(1)}, f32[6,96,256]{2,1,0:T(8,128)}, u32[]{:S(2)}) copy-start(f32[6,96,256]{2,1,0:T(8,128)} %spread_grads.3.halo_ref) | copy-start | bytes 1769476
  39.2 16.9 %all-to-all-start = ((bf16[4,288,256]{2,1,0:T(8,128)(2,1)}), bf16[4,288,256]{2,1,0:T(8,128)(2,1)S(1)}, u32[]{:S(2)}, u32[]{:S(2)}) async-start(bf16[4,288,256]{2,1,0:T(8,128)(2,1)} %pad_maximum_fusion), calls=%async_computation | async-start | bytes 1179648 | tf_op jit(solution)/shard_map/all_to_all | solution.py:300
  106.1 38.7 %all-to-all-start.1 = ((f32[16,6,2592]{2,1,0:T(8,128)}), f32[16,6,2592]{2,1,0:T(8,128)S(1)}, u32[]{:S(2)}, u32[]{:S(2)}) async-start(f32[16,6,2592]{2,1,0:T(8,128)} %get-tuple-element.24), calls=%async_computation.1 | async-start | bytes 2752512 | tf_op jit(solution)/shard_map/all_to_all | solution.py:367
  118.2 17.1 %collective-permute-start.2 = (bf16[1,192,256]{2,1,0:T(8,128)(2,1)S(1)}, bf16[1,192,256]{2,1,0:T(8,128)(2,1)S(1)}, u32[]{:S(2)}, u32[]{:S(2)}) collective-permute-start(bf16[1,192,256]{2,1,0:T(8,128)(2,1)S(1)} %get-tuple-element.34), channel_id=1, source_target_pairs={{0,1},{1,2},{2,3},{4,5},{5,6},{6,7},{8,9},{9,10},{10,11},{12,13},{... | collective-permute-start | bytes 294920 | tf_op jit(solution)/shard_map/ppermute | solution.py:310
  121.6 13.8 %collective-permute-start.3 = (bf16[1,192,256]{2,1,0:T(8,128)(2,1)S(1)}, bf16[1,192,256]{2,1,0:T(8,128)(2,1)S(1)}, u32[]{:S(2)}, u32[]{:S(2)}) collective-permute-start(bf16[1,192,256]{2,1,0:T(8,128)(2,1)S(1)} %get-tuple-element.35), channel_id=1, source_target_pairs={{1,0},{2,1},{3,2},{5,4},{6,5},{7,6},{9,8},{10,9},{11,10},{13,12},{... | collective-permute-start | bytes 294920 | tf_op jit(solution)/shard_map/ppermute | solution.py:310
  145.7 16.8 %all-to-all-start.2 = ((f32[4,6,2592]{2,1,0:T(8,128)}), f32[4,6,2592]{2,1,0:T(8,128)S(1)}, u32[]{:S(2)}, u32[]{:S(2)}) async-start(f32[4,6,2592]{2,1,0:T(8,128)} %broadcast_in_dim.3), calls=%async_computation.2 | async-start | bytes 688128 | tf_op jit(solution)/shard_map/all_to_all | solution.py:371

commit v4 on v3

--- a/solution.py
+++ b/solution.py
@@ -359,7 +359,7 @@
 
     w_scale = 1.0 / math.sqrt(slots * peers * layers)
     cotangent, w_term = lax.optimization_barrier((cotangent, w_term))
-    middle = 2 * offsets // 3
+    middle = offsets - GROUP
     own_grad = spread_grads(
         weight, index, cotangent, 0, own_count, offsets // 3, middle, start=own_grad
     )

time: 164 us -> 159 us (0.970)
  waiting for transfers between devices: 8.92 us -> 1.52 us
    all_to_all x1, waiting for transfers between devices: 8.77 us -> 1.51 us  [on_device(): terms = lax.all_to_all(w_term, ('xy', 'gz'), 0, 0, tiled=True)]
    pallas_call x3, Pallas kernels: 47 us -> 53.1 us  [spread_grads(): pl.pallas_call(functools.partial(spread_kernel, first, begin), grid=(step...]
    pallas_call x1, Pallas kernels: 12.5 us -> 6.83 us  [spread_last(): pl.pallas_call(functools.partial(spread_last_kernel, begin), grid=(steps...]
  transfers between devices with their start and end apart: 7 -> 7, of which waited for: 2 -> 1; matrix products, arithmetic and copies ran while one was open for 3% -> 4% of each run, Pallas kernels for 39% -> 40%
where the time goes in v4:
time: 159 us; the launch traced here: 158 us
  Pallas kernels  117 us (74%)
  starting transfers between devices  26.7 us (17%)
  local copies, waits for them, and re-layouts  7.93 us (5%)
  other arithmetic  4.51 us (3%)
    pallas_call x3, Pallas kernels, spread_grads(): pl.pallas_call(functools.partial(spread_kernel, first, begin), grid=(step...  53.1 us
    pallas_call x1, Pallas kernels, convolve(): pl.pallas_call(conv_kernel, grid=(offsets // GROUP,), in_specs=[whole(own...  49.3 us
    ppermute x2, starting transfers between devices, shift_z(): lax.ppermute(high_bound, 'gz', up)  7.01 us
    all_to_all x1, starting transfers between devices, on_device(): terms = lax.all_to_all(w_term, ('xy', 'gz'), 0, 0, tiled=True)  6.87 us
    pallas_call x1, Pallas kernels, spread_last(): pl.pallas_call(functools.partial(spread_last_kernel, begin), grid=(steps...  6.83 us
    all_to_all x1, starting transfers between devices, exchange(): got = lax.all_to_all(flat, 'xy', split_axis=0, concat_axis=0, tiled=True)  4.64 us
    pallas_call x2, Pallas kernels, pick_blocks(): pl.pallas_call(pick_kernel, out_shape=jax.ShapeDtypeStruct((width // LO,...  4.44 us
    all_to_all x1, starting transfers between devices, on_device(): rows = lax.all_to_all(spread_out, 'gz', 0, 0, tiled=True)  4.29 us
  transfers between devices with their start and end apart: 7, of which 1 were waited for; matrix products, arithmetic and copies ran while one was open for 4% of the time, Pallas kernels for 40%

profile of v4, /device:TPU:17, one launch (start us, length us, event | category | flops | bytes accessed | tf_op | source)
XLA Modules:
  0.0 158.3 jit_solution(3410707359291034110)
XLA Ops:
  0.6 2.0 %pick_columns.2 = bf16[2,96,256]{2,1,0:T(8,128)(2,1)} custom-call(bf16[96,2048]{1,0:T(8,128)(2,1)} %own_ref.1, s32[1,512]{1,0:T(1,128)} %bitcast.16), custom_call_target="tpu_custom_call" | custom-call | tf_op jit(solution)/shard_map/pick_columns/pallas_call | solution.py:80
  2.6 0.8 fusion.1
  3.5 3.7 %collective-permute-start = (bf16[1,96,256]{2,1,0:T(8,128)(2,1)S(1)}, bf16[1,96,256]{2,1,0:T(8,128)(2,1)S(1)}, u32[]{:S(2)}, u32[]{:S(2)}) collective-permute-start(bf16[1,96,256]{2,1,0:T(8,128)(2,1)S(1)} %get-tuple-element.33), channel_id=1, source_target_pairs={{0,1},{1,2},{2,3},{4,5},{5,6},{6,7},{8,9},{9,10},{10,11},{12,13},{... | collective-permute-start | bytes 147464 | tf_op jit(solution)/shard_map/ppermute | solution.py:310
  7.2 1.9 %collective-permute-start.1 = (bf16[1,96,256]{2,1,0:T(8,128)(2,1)S(1)}, bf16[1,96,256]{2,1,0:T(8,128)(2,1)S(1)}, u32[]{:S(2)}, u32[]{:S(2)}) collective-permute-start(bf16[1,96,256]{2,1,0:T(8,128)(2,1)S(1)} %get-tuple-element.34), channel_id=1, source_target_pairs={{1,0},{2,1},{3,2},{5,4},{6,5},{7,6},{9,8},{10,9},{11,10},{13,12},{... | collective-permute-start | bytes 147464 | tf_op jit(solution)/shard_map/ppermute | solution.py:310
  9.1 24.1 %spread_grads.3.halo_ref = f32[6,96,256]{2,1,0:T(8,128)} custom-call(bf16[2592,96]{1,0:T(8,128)(2,1)} %bitcast.9, s32[27,2048]{1,0:T(8,128)} %index_ref.9, bf16[96,2048]{1,0:T(8,128)(2,1)} %up_ref.4), custom_call_target="tpu_custom_call" | custom-call | flops 17326669824 | bytes 2097152 | tf_op jit(solution)/shard_map/spread_grads/pallas_call | solution.py:218
  33.1 0.0 collective-permute-done
  33.1 0.0 collective-permute-done.1
  33.2 0.7 pad_maximum_fusion.2.refs_1_.z_ref
  33.8 1.2 subtract_convert_fusion
  35.0 2.4 %pick_columns.3 = bf16[4,96,256]{2,1,0:T(8,128)(2,1)} custom-call(bf16[96,2048]{1,0:T(8,128)(2,1)} %own_ref.1, bf16[2,96,256]{2,1,0:T(8,128)(2,1)} %pad_maximum_fusion.2.refs_1_.z_ref, s32[1,1024]{1,0:T(1,128)} %bitcast.14), custom_call_target="tpu_custom_call" | custom-call | tf_op jit(solution)/shard_map/pick_columns/pallas_call | solution.py:80
  37.4 0.0 copy-start
  37.4 1.8 %pad_maximum_fusion = bf16[4,288,256]{2,1,0:T(8,128)(2,1)} fusion(bf16[4,96,256]{2,1,0:T(8,128)(2,1)S(1)} %get-tuple-element.29, bf16[4,96,256]{2,1,0:T(8,128)(2,1)S(1)} %get-tuple-element.30, bf16[4,96,256]{2,1,0:T(8,128)(2,1)} %pick_columns.3), kind=kLoop, calls=%fused_computation | loop fusion | flops 1769472 | bytes 1179648 | tf_op jit(solution)/shard_map/concatenate | solution.py:337
  39.3 4.6 %all-to-all-start = ((bf16[4,288,256]{2,1,0:T(8,128)(2,1)}), bf16[4,288,256]{2,1,0:T(8,128)(2,1)S(1)}, u32[]{:S(2)}, u32[]{:S(2)}) async-start(bf16[4,288,256]{2,1,0:T(8,128)(2,1)} %pad_maximum_fusion), calls=%async_computation | async-start | bytes 1179648 | tf_op jit(solution)/shard_map/all_to_all | solution.py:300
  43.9 0.0 copy-done
  43.9 0.7 slice.34
  44.6 1.1 copy.10.wt_ref
  45.7 11.3 %spread_grads.4.refs_0_ = f32[8,96,256]{2,1,0:T(8,128)} custom-call(bf16[864,96]{1,0:T(8,128)(2,1)} %bitcast.12, s32[27,2048]{1,0:T(8,128)} %index_ref.9, bf16[96,2048]{1,0:T(8,128)(2,1)} %up_ref.4), custom_call_target="tpu_custom_call" | custom-call | flops 7587495936 | bytes 2097152 | tf_op jit(solution)/shard_map/spread_grads/pallas_call | solution.py:218
  57.0 0.0 all-to-all-done
  57.0 0.7 slice.42.xy_ref
  57.7 49.3 %convolve.1 = (bf16[96,2048]{1,0:T(8,128)(2,1)}, f32[16,6,2592]{2,1,0:T(8,128)}) custom-call(bf16[96,2048]{1,0:T(8,128)(2,1)} %own_ref.1, bf16[2,96,256]{2,1,0:T(8,128)(2,1)} %pad_maximum_fusion.2.refs_1_.z_ref, bf16[4,96,256]{2,1,0:T(8,128)(2,1)} %slice.42.xy_ref, bf16[96,2592]{1,0:T(8,128)(2,1)} %copy.10.wt_ref, s32[27,2048]{1,0:T(8,128)} %index_ref.9, ...), custom_call_target="tpu_custom_call" | custom-call | flops 40089157632 | bytes 4194304 | tf_op jit(solution)/shard_map/convolve/pallas_call | solution.py:118
  107.0 6.9 %all-to-all-start.1 = ((f32[16,6,2592]{2,1,0:T(8,128)}), f32[16,6,2592]{2,1,0:T(8,128)S(1)}, u32[]{:S(2)}, u32[]{:S(2)}) async-start(f32[16,6,2592]{2,1,0:T(8,128)} %get-tuple-element.24), calls=%async_computation.1 | async-start | bytes 2752512 | tf_op jit(solution)/shard_map/all_to_all | solution.py:367
  113.8 0.8 slice.36
  114.6 0.6 slice.35
  115.2 0.8 slice.43.pairs_ref
  116.0 3.3 %halo_add.1 = (f32[8,96,256]{2,1,0:T(8,128)}, bf16[2,192,256]{2,1,0:T(8,128)(2,1)}) custom-call(bf16[4,192,256]{2,1,0:T(8,128)(2,1)} %slice.43.pairs_ref, s32[1,1024]{1,0:T(1,128)} %bitcast.15, f32[6,96,256]{2,1,0:T(8,128)} %spread_grads.3.halo_ref), custom_call_target="tpu_custom_call" | custom-call | tf_op jit(solution)/shard_map/halo_add/pallas_call | solution.py:283
  119.3 1.0 fusion
  120.3 3.3 %collective-permute-start.2 = (bf16[1,192,256]{2,1,0:T(8,128)(2,1)S(1)}, bf16[1,192,256]{2,1,0:T(8,128)(2,1)S(1)}, u32[]{:S(2)}, u32[]{:S(2)}) collective-permute-start(bf16[1,192,256]{2,1,0:T(8,128)(2,1)S(1)} %get-tuple-element.31), channel_id=1, source_target_pairs={{0,1},{1,2},{2,3},{4,5},{5,6},{6,7},{8,9},{9,10},{10,11},{12,13},{... | collective-permute-start | bytes 294920 | tf_op jit(solution)/shard_map/ppermute | solution.py:310
  123.6 1.9 %collective-permute-start.3 = (bf16[1,192,256]{2,1,0:T(8,128)(2,1)S(1)}, bf16[1,192,256]{2,1,0:T(8,128)(2,1)S(1)}, u32[]{:S(2)}, u32[]{:S(2)}) collective-permute-start(bf16[1,192,256]{2,1,0:T(8,128)(2,1)S(1)} %get-tuple-element.32), channel_id=1, source_target_pairs={{1,0},{2,1},{3,2},{5,4},{6,5},{7,6},{9,8},{10,9},{11,10},{13,12},{... | collective-permute-start | bytes 294920 | tf_op jit(solution)/shard_map/ppermute | solution.py:310
  125.6 17.8 %spread_grads.5.start_ref = f32[8,96,256]{2,1,0:T(8,128)} custom-call(bf16[1440,96]{1,0:T(8,128)(2,1)} %bitcast.11, s32[27,2048]{1,0:T(8,128)} %index_ref.9, bf16[96,2048]{1,0:T(8,128)(2,1)} %up_ref.4, f32[8,96,256]{2,1,0:T(8,128)} %spread_grads.4.refs_0_), custom_call_target="tpu_custom_call" | custom-call | flops 12645826560 | bytes 2097152 | tf_op jit(solution)/shard_map/spread_grads/pallas_call | solution.py:218
  143.3 0.0 collective-permute-done.2
  143.3 0.0 collective-permute-done.3
  143.3 0.7 pad_maximum_fusion.1.z_ref
  144.0 1.5 all-to-all-done.1
  145.5 0.1 reduce_sum.9
  145.6 0.8 broadcast_in_dim.3
  146.4 4.3 %all-to-all-start.2 = ((f32[4,6,2592]{2,1,0:T(8,128)}), f32[4,6,2592]{2,1,0:T(8,128)S(1)}, u32[]{:S(2)}, u32[]{:S(2)}) async-start(f32[4,6,2592]{2,1,0:T(8,128)} %broadcast_in_dim.3), calls=%async_computation.2 | async-start | bytes 688128 | tf_op jit(solution)/shard_map/all_to_all | solution.py:371
  150.7 6.8 %spread_last.1 = f32[96,2048]{1,0:T(8,128)} custom-call(bf16[288,96]{1,0:T(8,128)(2,1)} %bitcast.13, s32[27,2048]{1,0:T(8,128)} %index_ref.9, bf16[96,2048]{1,0:T(8,128)(2,1)} %up_ref.4, f32[8,96,256]{2,1,0:T(8,128)} %spread_grads.5.start_ref, f32[8,96,256]{2,1,0:T(8,128)} %get-tuple-element.26.ext_ref, bf16[2,192,256]{2,1,0:T(8,128)(2,1)} %pad_maximum_fusion.1.z_ref, ...), custom_call_target="tpu_custom_call" | custom-call | flops 2529165312 | bytes 2097152 | tf_op jit(solution)/shard_map/spread_last/pallas_call | solution.py:235
  157.5 0.0 all-to-all-done.2
  157.5 0.7 reshape.29
  (1 shorter events, 0.0 us)
Async XLA Ops:
  3.5 29.7 %collective-permute-start = (bf16[1,96,256]{2,1,0:T(8,128)(2,1)S(1)}, bf16[1,96,256]{2,1,0:T(8,128)(2,1)S(1)}, u32[]{:S(2)}, u32[]{:S(2)}) collective-permute-start(bf16[1,96,256]{2,1,0:T(8,128)(2,1)S(1)} %get-tuple-element.33), channel_id=1, source_target_pairs={{0,1},{1,2},{2,3},{4,5},{5,6},{6,7},{8,9},{9,10},{10,11},{12,13},{... | collective-permute-start | bytes 147464 | tf_op jit(solution)/shard_map/ppermute | solution.py:310
  7.2 26.0 %collective-permute-start.1 = (bf16[1,96,256]{2,1,0:T(8,128)(2,1)S(1)}, bf16[1,96,256]{2,1,0:T(8,128)(2,1)S(1)}, u32[]{:S(2)}, u32[]{:S(2)}) collective-permute-start(bf16[1,96,256]{2,1,0:T(8,128)(2,1)S(1)} %get-tuple-element.34), channel_id=1, source_target_pairs={{1,0},{2,1},{3,2},{5,4},{6,5},{7,6},{9,8},{10,9},{11,10},{13,12},{... | collective-permute-start | bytes 147464 | tf_op jit(solution)/shard_map/ppermute | solution.py:310
  37.4 6.5 %copy-start = (bf16[27,96,96]{2,1,0:T(8,128)(2,1)S(1)}, bf16[27,96,96]{2,1,0:T(8,128)(2,1)}, u32[]{:S(2)}) copy-start(bf16[27,96,96]{2,1,0:T(8,128)(2,1)} %param.7) | copy-start | bytes 1492996
  39.3 17.7 %all-to-all-start = ((bf16[4,288,256]{2,1,0:T(8,128)(2,1)}), bf16[4,288,256]{2,1,0:T(8,128)(2,1)S(1)}, u32[]{:S(2)}, u32[]{:S(2)}) async-start(bf16[4,288,256]{2,1,0:T(8,128)(2,1)} %pad_maximum_fusion), calls=%async_computation | async-start | bytes 1179648 | tf_op jit(solution)/shard_map/all_to_all | solution.py:300
  107.0 38.6 %all-to-all-start.1 = ((f32[16,6,2592]{2,1,0:T(8,128)}), f32[16,6,2592]{2,1,0:T(8,128)S(1)}, u32[]{:S(2)}, u32[]{:S(2)}) async-start(f32[16,6,2592]{2,1,0:T(8,128)} %get-tuple-element.24), calls=%async_computation.1 | async-start | bytes 2752512 | tf_op jit(solution)/shard_map/all_to_all | solution.py:367
  120.3 23.0 %collective-permute-start.2 = (bf16[1,192,256]{2,1,0:T(8,128)(2,1)S(1)}, bf16[1,192,256]{2,1,0:T(8,128)(2,1)S(1)}, u32[]{:S(2)}, u32[]{:S(2)}) collective-permute-start(bf16[1,192,256]{2,1,0:T(8,128)(2,1)S(1)} %get-tuple-element.31), channel_id=1, source_target_pairs={{0,1},{1,2},{2,3},{4,5},{5,6},{6,7},{8,9},{9,10},{10,11},{12,13},{... | collective-permute-start | bytes 294920 | tf_op jit(solution)/shard_map/ppermute | solution.py:310
  123.6 19.7 %collective-permute-start.3 = (bf16[1,192,256]{2,1,0:T(8,128)(2,1)S(1)}, bf16[1,192,256]{2,1,0:T(8,128)(2,1)S(1)}, u32[]{:S(2)}, u32[]{:S(2)}) collective-permute-start(bf16[1,192,256]{2,1,0:T(8,128)(2,1)S(1)} %get-tuple-element.32), channel_id=1, source_target_pairs={{1,0},{2,1},{3,2},{5,4},{6,5},{7,6},{9,8},{10,9},{11,10},{13,12},{... | collective-permute-start | bytes 294920 | tf_op jit(solution)/shard_map/ppermute | solution.py:310
  146.4 11.1 %all-to-all-start.2 = ((f32[4,6,2592]{2,1,0:T(8,128)}), f32[4,6,2592]{2,1,0:T(8,128)S(1)}, u32[]{:S(2)}, u32[]{:S(2)}) async-start(f32[4,6,2592]{2,1,0:T(8,128)} %broadcast_in_dim.3), calls=%async_computation.2 | async-start | bytes 688128 | tf_op jit(solution)/shard_map/all_to_all | solution.py:371
